TPU v7x, 512 devices: a whole 4x8x8 slice. The times are simulated.
512 devices in a mesh: blk: 8 (over y_hi, core), grp: 64 (over y_lo, x, z).
Axes of the slice: x: 4, y: 8 (y_hi: 4, y_lo: 2; y = y_hi * 2 + y_lo), z: 8, core: 2. Of those that a mesh axis runs over, the one named last changes fastest.
Arguments:
- patches: bfloat16 [393216, 1152], P(('blk', 'grp')), may hold values from -6 to 6
- segment_ids: int32 [512, 768], P(('blk', 'grp')), may hold values from 0 to 2, never falling along the last dimension, each value on 1 to 512 neighbouring positions
- image_ids: int32 [1536], P(('blk', 'grp')), may hold values from 0 to 1535, each once
- text_embeds: bfloat16 [1536, 1152], P(('blk', 'grp')), may hold values from -6 to 6
- key_weight: bfloat16 [1152, 1152], P('grp'), may hold values from -0.1875 to 0.1875
- value_weight: bfloat16 [1152, 1152], P('grp'), may hold values from -0.1875 to 0.1875
- pool_query: bfloat16 [1152], replicated, may hold values from -110 to 110
- logit_scale: float32 [1], replicated, may hold values from 90 to 110
- logit_bias: float32 [1], replicated, may hold values from -9 to -7
Outputs:
- image_grad: float32 [1536, 1152], P(('blk', 'grp'))
- text_grad: float32 [1536, 1152], P(('blk', 'grp'))
Inputs may be any that keep to these rules, and one draw needn't show every extreme that they name: `segment_ids`: the rows of each image slot of a device form one run; every slot holds at least one row and one slot of every device exactly 512. `image_ids`: every pair index appears exactly once.
All inputs are finite; a program needn't handle non-finite values.
Results may differ from a plain program's by a relative error of at most 0.018.
The roundings to bfloat16 on the way count: a program that leaves them out, or rounds other values in their place, can miss the bound.
Values may be sent and summed in bfloat16 or wider, within the bound.
No kernel may reach another device: no remote copies, remote signals or barrier semaphores. Data moves between devices by JAX's collectives and lax.ppermute only.
A program may use at most 64 MiB of HBM per device.

v0:
```python
import math

import jax
import jax.numpy as jnp
from jax import lax
from jax.sharding import PartitionSpec as P

D = 1152
HEADS = 16
HEAD_DIM = 72
IMG_DEV = 3


def from_behind(shard, axis, by):
    peers = lax.axis_size(axis)
    return lax.ppermute(shard, axis, [(i, (i + by) % peers) for i in range(peers)])


def pool_images(patches, segments, key_full, value_full, pool_query):
    key_rows = jnp.dot(patches, key_full, preferred_element_type=jnp.float32).astype(jnp.bfloat16)
    value_rows = jnp.dot(patches, value_full, preferred_element_type=jnp.float32).astype(
        jnp.bfloat16
    )
    row_count = patches.shape[0]
    query = pool_query.reshape(HEADS, HEAD_DIM)
    scores = jnp.einsum(
        "rhe,he->rh",
        key_rows.reshape(row_count, HEADS, HEAD_DIM),
        query,
        preferred_element_type=jnp.float32,
    ) / math.sqrt(HEAD_DIM)
    slot_mask = segments[None, :] == jnp.arange(IMG_DEV, dtype=jnp.int32)[:, None]
    masked = jnp.where(slot_mask[:, :, None], scores[None, :, :], -1e30)
    peak_score = jnp.max(masked, axis=1, keepdims=True)
    powers = jnp.where(slot_mask[:, :, None], jnp.exp(masked - peak_score), 0.0)
    weights = (powers / jnp.sum(powers, axis=1, keepdims=True)).astype(jnp.bfloat16)
    pooled = jnp.einsum(
        "srh,rhe->she",
        weights,
        value_rows.reshape(row_count, HEADS, HEAD_DIM),
        preferred_element_type=jnp.float32,
    )
    return pooled.reshape(IMG_DEV, D)


def image_terms(text_block, first_index, image_low, pair_ids, scale, offset, pair_total):
    row_count = text_block.shape[0]
    logits = (
        scale
        * lax.dot_general(
            image_low, text_block, (((1,), (1,)), ((), ())), preferred_element_type=jnp.float32
        )
        + offset
    )
    columns = first_index + jnp.arange(row_count, dtype=jnp.int32)
    pair_sign = jnp.where(pair_ids[:, None] == columns[None, :], 1.0, -1.0)
    return (scale * (-pair_sign * jax.nn.sigmoid(-pair_sign * logits) / pair_total)).astype(
        jnp.bfloat16
    )


def visit(text_block, first_index, image_low, pair_ids, scale, offset, pair_total):
    scaled = image_terms(text_block, first_index, image_low, pair_ids, scale, offset, pair_total)
    image_part = jnp.dot(scaled, text_block, preferred_element_type=jnp.float32)
    text_part = lax.dot_general(
        scaled, image_low, (((0,), (0,)), ((), ())), preferred_element_type=jnp.float32
    )
    return (image_part, text_part)


def body(
    patches,
    segment_ids,
    image_ids,
    text_embeds,
    key_weight,
    value_weight,
    pool_query,
    logit_scale,
    logit_bias,
):
    key_full, value_full = (
        lax.all_gather(key_weight, "grp", axis=0, tiled=True),
        lax.all_gather(value_weight, "grp", axis=0, tiled=True),
    )
    pooled = pool_images(patches, segment_ids[0], key_full, value_full, pool_query)
    image_norm = jnp.sqrt(jnp.sum(pooled * pooled, axis=1, keepdims=True) + 1e-06)
    unit_image = pooled / image_norm
    image_low = unit_image.astype(jnp.bfloat16)
    text_full = text_embeds.astype(jnp.float32)
    text_norm = jnp.sqrt(jnp.sum(text_full * text_full, axis=1, keepdims=True) + 1e-06)
    unit_text = text_full / text_norm
    text_low = unit_text.astype(jnp.bfloat16)
    group_count = lax.axis_size("blk")
    member_count = lax.axis_size("grp")
    my_group = lax.axis_index("blk")
    pair_total = IMG_DEV * group_count * member_count
    group_rows = IMG_DEV * member_count
    scale = logit_scale[0]
    offset = logit_bias[0]
    width = text_low.shape[1]
    image_acc = jnp.zeros((IMG_DEV, width), jnp.float32)
    group_block = lax.all_gather(text_low, "grp", axis=0, tiled=True)

    def step_one(visit_index, carry):
        text_block, grad_block, image_sum = carry
        owner_group = (my_group - visit_index) % group_count
        image_one, text_one = visit(
            text_block, owner_group * group_rows, image_low, image_ids, scale, offset, pair_total
        )
        grad_block = from_behind(grad_block + text_one, "blk", 1)
        text_block = from_behind(text_block, "blk", 1)
        return (text_block, grad_block, image_sum + image_one)

    start = (group_block, jnp.zeros((group_rows, width), jnp.float32), image_acc)
    text_block, grad_block, image_acc = lax.fori_loop(0, group_count - 1, step_one, start)
    last_owner = (my_group - (group_count - 1)) % group_count
    image_one, text_one = visit(
        text_block, last_owner * group_rows, image_low, image_ids, scale, offset, pair_total
    )
    group_grad = from_behind(grad_block + text_one, "blk", 1)
    image_acc = image_acc + image_one
    text_part = lax.psum_scatter(group_grad, "grp", scatter_dimension=0, tiled=True)
    text_grad = (
        text_part - unit_text * jnp.sum(unit_text * text_part, axis=1, keepdims=True)
    ) / text_norm
    image_grad = (
        image_acc - unit_image * jnp.sum(unit_image * image_acc, axis=1, keepdims=True)
    ) / image_norm
    return (image_grad, text_grad)


def solution(mesh):
    in_specs = (
        P(("blk", "grp"), None),
        P(("blk", "grp"), None),
        P(("blk", "grp")),
        P(("blk", "grp"), None),
        P("grp", None),
        P("grp", None),
        P(),
        P(),
        P(),
    )
    out_specs = (P(("blk", "grp"), None), P(("blk", "grp"), None))
    return jax.shard_map(body, mesh=mesh, in_specs=in_specs, out_specs=out_specs, check_vma=False)
```

profile of v0, /device:TPU:56, one launch (start us, length us, event | category | flops | bytes accessed | tf_op | source)
XLA Modules:
  0.0 1527.4 jit_solution(6853908318358241821)
XLA Ops:
  11.8 165.5 %all-gather = bf16[64,3,1152]{2,1,0:T(4,128)(2,1)S(1)} all-gather(bf16[1,3,1152]{2,1,0:T(4,128)(2,1)S(1)} %convert_bitcast_fusion), channel_id=1, replica_groups=mesh['blk'=8,'grp'=64] {'grp'}, dimensions={0}, use_global_device_ids=true | all-gather | bytes 449280 | tf_op jit(solution)/shard_map/all_gather | solution.py:103
  179.6 141.0 %all-gather.8.cloned.1.call-done = bf16[64,18,1152]{2,1,0:T(8,128)(2,1)} async-done(((bf16[1,18,1152]{2,1,0:T(8,128)(2,1)}), bf16[64,18,1152]{2,1,0:T(8,128)(2,1)}) %all-gather.8.cloned.1.call-update) | async-done | bytes 2654224 | tf_op jit(solution)/shard_map/all_gather | solution.py:83
  320.7 5.4 reshape.72
  326.1 5.5 convolution_convert_fusion
  331.6 3.9 copy.16
  335.5 1.8 fusion.42
  337.3 288.7 %all-gather.6.cloned.1.call-done = bf16[64,18,1152]{2,1,0:T(8,128)(2,1)} async-done(((bf16[1,18,1152]{2,1,0:T(8,128)(2,1)}), bf16[64,18,1152]{2,1,0:T(8,128)(2,1)}) %all-gather.6.cloned.1.call-update) | async-done | bytes 2654224 | tf_op jit(solution)/shard_map/all_gather | solution.py:84
  626.1 5.4 reshape.70
  631.4 5.5 convolution_convert_fusion.1
  637.0 3.9 copy.15
  641.1 2.2 multiply_reduce_fusion
  644.2 229.5 %while.20 = (s32[]{:T(128)}, bf16[192,1152]{1,0:T(8,128)(2,1)S(1)}, f32[192,1152]{1,0:T(8,128)S(1)}, f32[3,1152]{1,0:T(4,128)}, s32[3]{0:T(128)}, /*index=5*/s32...) while((s32[]{:T(128)}, bf16[192,1152]{1,0:T(8,128)(2,1)S(1)}, ...), condition=%wide.region_5.6_spmd.clone, body=%wide.region_4.5_spmd.clone.sunk | while | flops 4216528 | bytes 8894216 | solution.py:116
  644.3 2.2 fusion.75
  647.8 1.9 collective-permute-start.1
  649.7 2.4 collective-permute-start
  652.9 29.4 %collective-permute-done = bf16[192,1152]{1,0:T(8,128)(2,1)S(1)} collective-permute-done((bf16[192,1152]{1,0:T(8,128)(2,1)S(1)}, bf16[192,1152]{1,0:T(8,128)(2,1)S(1)}, u32[]{:S(2)}, u32[]{:S(2)}) %collective-permute-start) | collective-permute-done | bytes 442400 | tf_op jit(solution)/shard_map/while/body/eval_jaxpr/ppermute | solution.py:16
  682.4 2.2 fusion.75
  685.9 1.9 collective-permute-start.1
  687.8 3.6 collective-permute-start
  691.4 1.5 convolution_add_fusion.7
  692.9 20.7 %collective-permute-done = bf16[192,1152]{1,0:T(8,128)(2,1)S(1)} collective-permute-done((bf16[192,1152]{1,0:T(8,128)(2,1)S(1)}, bf16[192,1152]{1,0:T(8,128)(2,1)S(1)}, u32[]{:S(2)}, u32[]{:S(2)}) %collective-permute-start) | collective-permute-done | bytes 442400 | tf_op jit(solution)/shard_map/while/body/eval_jaxpr/ppermute | solution.py:16
  713.6 2.2 fusion.75
  717.1 1.9 collective-permute-start.1
  719.0 2.9 collective-permute-start
  721.9 1.5 convolution_add_fusion.7
  723.4 15.5 %collective-permute-done = bf16[192,1152]{1,0:T(8,128)(2,1)S(1)} collective-permute-done((bf16[192,1152]{1,0:T(8,128)(2,1)S(1)}, bf16[192,1152]{1,0:T(8,128)(2,1)S(1)}, u32[]{:S(2)}, u32[]{:S(2)}) %collective-permute-start) | collective-permute-done | bytes 442400 | tf_op jit(solution)/shard_map/while/body/eval_jaxpr/ppermute | solution.py:16
  739.0 2.2 fusion.75
  742.5 1.9 collective-permute-start.1
  744.4 5.7 collective-permute-start
  750.1 1.5 convolution_add_fusion.7
  751.6 11.3 collective-permute-done
  762.9 2.2 fusion.75
  766.4 16.3 %collective-permute-start.1 = (f32[192,1152]{1,0:T(8,128)}, f32[192,1152]{1,0:T(8,128)S(1)}, u32[]{:S(2)}, u32[]{:S(2)}) collective-permute-start(f32[192,1152]{1,0:T(8,128)} %convolution_add_fusion.6), channel_id=1, source_target_pairs={{0,64},{64,128},{128,192},{192,256},{256,320},{320,384},{384,448},... | collective-permute-start | bytes 2654216 | tf_op jit(solution)/shard_map/while/body/eval_jaxpr/ppermute | solution.py:16
  782.8 6.6 collective-permute-start
  789.4 1.5 convolution_add_fusion.7
  790.9 2.5 collective-permute-done
  793.4 2.2 fusion.75
  796.9 24.4 %collective-permute-start.1 = (f32[192,1152]{1,0:T(8,128)}, f32[192,1152]{1,0:T(8,128)S(1)}, u32[]{:S(2)}, u32[]{:S(2)}) collective-permute-start(f32[192,1152]{1,0:T(8,128)} %convolution_add_fusion.6), channel_id=1, source_target_pairs={{0,64},{64,128},{128,192},{192,256},{256,320},{320,384},{384,448},... | collective-permute-start | bytes 2654216 | tf_op jit(solution)/shard_map/while/body/eval_jaxpr/ppermute | solution.py:16
  821.4 6.6 collective-permute-start
  829.4 11.3 collective-permute-done
  840.8 2.2 fusion.75
  844.3 8.9 collective-permute-start.1
  853.2 6.6 collective-permute-start
  861.3 12.4 collective-permute-done
  875.0 12.3 collective-permute-start.2
  887.3 16.4 %collective-permute-done.2 = f32[192,1152]{1,0:T(8,128)S(1)} collective-permute-done((f32[192,1152]{1,0:T(8,128)S(1)}, f32[192,1152]{1,0:T(8,128)S(1)}, u32[]{:S(2)}, u32[]{:S(2)}) %collective-permute-start.2) | collective-permute-done | bytes 884768 | tf_op jit(solution)/shard_map/ppermute | solution.py:16
  907.6 610.6 %all-reduce.3.cloned.1.call-done = f32[192,1152]{1,0:T(8,128)} async-done(((f32[192,1152]{1,0:T(8,128)}), f32[192,1152]{1,0:T(8,128)}) %all-reduce.3.cloned.1.call-update) | async-done | bytes 884752
  1519.3 1.6 subtract_divide_fusion
  (77 shorter events, 25.3 us)
Async XLA Ops:
  7.2 318.9 %copy-start = (bf16[768,1152]{1,0:T(8,128)(2,1)S(1)}, bf16[768,1152]{1,0:T(8,128)(2,1)}, u32[]{:S(2)}) copy-start(bf16[768,1152]{1,0:T(8,128)(2,1)} %param.11) | copy-start | bytes 5308420
  7.2 313.5 %all-gather.8.cloned.1.call-start = ((), (), s32[]{:S(2)}) async-start(), calls=%async_computation.1 | async-start | bytes 3594240 | tf_op jit(solution)/shard_map/all_gather | solution.py:83
  7.9 618.1 %all-gather.6.cloned.1.call-start = ((), (), s32[]{:S(2)}) async-start(), calls=%async_computation | async-start | bytes 3594240 | tf_op jit(solution)/shard_map/all_gather | solution.py:84
  8.7 1509.6 %all-reduce.3.cloned.1.call-start = ((), (), s32[]{:S(2)}) async-start(), calls=%async_computation.2 | async-start | bytes 1769472
  11.1 0.8 copy-start.5
  643.3 0.8 copy-start.7
  647.8 34.6 %collective-permute-start.1 = (f32[192,1152]{1,0:T(8,128)}, f32[192,1152]{1,0:T(8,128)S(1)}, u32[]{:S(2)}, u32[]{:S(2)}) collective-permute-start(f32[192,1152]{1,0:T(8,128)} %convolution_add_fusion.6), channel_id=1, source_target_pairs={{0,64},{64,128},{128,192},{192,256},{256,320},{320,384},{384,448},... | collective-permute-start | bytes 2654216 | tf_op jit(solution)/shard_map/while/body/eval_jaxpr/ppermute | solution.py:16
  649.7 32.7 %collective-permute-start = (bf16[192,1152]{1,0:T(8,128)(2,1)S(1)}, bf16[192,1152]{1,0:T(8,128)(2,1)S(1)}, u32[]{:S(2)}, u32[]{:S(2)}) collective-permute-start(bf16[192,1152]{1,0:T(8,128)(2,1)S(1)} %copy.26), channel_id=1, source_target_pairs={{0,64},{64,128},{128,192},{192,256},{256,320},{320,384},{384,448},... | collective-permute-start | bytes 1327112 | tf_op jit(solution)/shard_map/while/body/eval_jaxpr/ppermute | solution.py:16
  685.9 27.7 %collective-permute-start.1 = (f32[192,1152]{1,0:T(8,128)}, f32[192,1152]{1,0:T(8,128)S(1)}, u32[]{:S(2)}, u32[]{:S(2)}) collective-permute-start(f32[192,1152]{1,0:T(8,128)} %convolution_add_fusion.6), channel_id=1, source_target_pairs={{0,64},{64,128},{128,192},{192,256},{256,320},{320,384},{384,448},... | collective-permute-start | bytes 2654216 | tf_op jit(solution)/shard_map/while/body/eval_jaxpr/ppermute | solution.py:16
  687.8 25.8 %collective-permute-start = (bf16[192,1152]{1,0:T(8,128)(2,1)S(1)}, bf16[192,1152]{1,0:T(8,128)(2,1)S(1)}, u32[]{:S(2)}, u32[]{:S(2)}) collective-permute-start(bf16[192,1152]{1,0:T(8,128)(2,1)S(1)} %copy.26), channel_id=1, source_target_pairs={{0,64},{64,128},{128,192},{192,256},{256,320},{320,384},{384,448},... | collective-permute-start | bytes 1327112 | tf_op jit(solution)/shard_map/while/body/eval_jaxpr/ppermute | solution.py:16
  717.1 21.8 %collective-permute-start.1 = (f32[192,1152]{1,0:T(8,128)}, f32[192,1152]{1,0:T(8,128)S(1)}, u32[]{:S(2)}, u32[]{:S(2)}) collective-permute-start(f32[192,1152]{1,0:T(8,128)} %convolution_add_fusion.6), channel_id=1, source_target_pairs={{0,64},{64,128},{128,192},{192,256},{256,320},{320,384},{384,448},... | collective-permute-start | bytes 2654216 | tf_op jit(solution)/shard_map/while/body/eval_jaxpr/ppermute | solution.py:16
  719.0 19.9 %collective-permute-start = (bf16[192,1152]{1,0:T(8,128)(2,1)S(1)}, bf16[192,1152]{1,0:T(8,128)(2,1)S(1)}, u32[]{:S(2)}, u32[]{:S(2)}) collective-permute-start(bf16[192,1152]{1,0:T(8,128)(2,1)S(1)} %copy.26), channel_id=1, source_target_pairs={{0,64},{64,128},{128,192},{192,256},{256,320},{320,384},{384,448},... | collective-permute-start | bytes 1327112 | tf_op jit(solution)/shard_map/while/body/eval_jaxpr/ppermute | solution.py:16
  742.5 20.4 %collective-permute-start.1 = (f32[192,1152]{1,0:T(8,128)}, f32[192,1152]{1,0:T(8,128)S(1)}, u32[]{:S(2)}, u32[]{:S(2)}) collective-permute-start(f32[192,1152]{1,0:T(8,128)} %convolution_add_fusion.6), channel_id=1, source_target_pairs={{0,64},{64,128},{128,192},{192,256},{256,320},{320,384},{384,448},... | collective-permute-start | bytes 2654216 | tf_op jit(solution)/shard_map/while/body/eval_jaxpr/ppermute | solution.py:16
  744.4 18.5 %collective-permute-start = (bf16[192,1152]{1,0:T(8,128)(2,1)S(1)}, bf16[192,1152]{1,0:T(8,128)(2,1)S(1)}, u32[]{:S(2)}, u32[]{:S(2)}) collective-permute-start(bf16[192,1152]{1,0:T(8,128)(2,1)S(1)} %copy.26), channel_id=1, source_target_pairs={{0,64},{64,128},{128,192},{192,256},{256,320},{320,384},{384,448},... | collective-permute-start | bytes 1327112 | tf_op jit(solution)/shard_map/while/body/eval_jaxpr/ppermute | solution.py:16
  766.4 27.0 %collective-permute-start.1 = (f32[192,1152]{1,0:T(8,128)}, f32[192,1152]{1,0:T(8,128)S(1)}, u32[]{:S(2)}, u32[]{:S(2)}) collective-permute-start(f32[192,1152]{1,0:T(8,128)} %convolution_add_fusion.6), channel_id=1, source_target_pairs={{0,64},{64,128},{128,192},{192,256},{256,320},{320,384},{384,448},... | collective-permute-start | bytes 2654216 | tf_op jit(solution)/shard_map/while/body/eval_jaxpr/ppermute | solution.py:16
  782.8 10.6 collective-permute-start
  796.9 43.9 %collective-permute-start.1 = (f32[192,1152]{1,0:T(8,128)}, f32[192,1152]{1,0:T(8,128)S(1)}, u32[]{:S(2)}, u32[]{:S(2)}) collective-permute-start(f32[192,1152]{1,0:T(8,128)} %convolution_add_fusion.6), channel_id=1, source_target_pairs={{0,64},{64,128},{128,192},{192,256},{256,320},{320,384},{384,448},... | collective-permute-start | bytes 2654216 | tf_op jit(solution)/shard_map/while/body/eval_jaxpr/ppermute | solution.py:16
  821.4 19.4 %collective-permute-start = (bf16[192,1152]{1,0:T(8,128)(2,1)S(1)}, bf16[192,1152]{1,0:T(8,128)(2,1)S(1)}, u32[]{:S(2)}, u32[]{:S(2)}) collective-permute-start(bf16[192,1152]{1,0:T(8,128)(2,1)S(1)} %copy.26), channel_id=1, source_target_pairs={{0,64},{64,128},{128,192},{192,256},{256,320},{320,384},{384,448},... | collective-permute-start | bytes 1327112 | tf_op jit(solution)/shard_map/while/body/eval_jaxpr/ppermute | solution.py:16
  844.3 29.4 %collective-permute-start.1 = (f32[192,1152]{1,0:T(8,128)}, f32[192,1152]{1,0:T(8,128)S(1)}, u32[]{:S(2)}, u32[]{:S(2)}) collective-permute-start(f32[192,1152]{1,0:T(8,128)} %convolution_add_fusion.6), channel_id=1, source_target_pairs={{0,64},{64,128},{128,192},{192,256},{256,320},{320,384},{384,448},... | collective-permute-start | bytes 2654216 | tf_op jit(solution)/shard_map/while/body/eval_jaxpr/ppermute | solution.py:16
  853.2 20.5 %collective-permute-start = (bf16[192,1152]{1,0:T(8,128)(2,1)S(1)}, bf16[192,1152]{1,0:T(8,128)(2,1)S(1)}, u32[]{:S(2)}, u32[]{:S(2)}) collective-permute-start(bf16[192,1152]{1,0:T(8,128)(2,1)S(1)} %copy.26), channel_id=1, source_target_pairs={{0,64},{64,128},{128,192},{192,256},{256,320},{320,384},{384,448},... | collective-permute-start | bytes 1327112 | tf_op jit(solution)/shard_map/while/body/eval_jaxpr/ppermute | solution.py:16
  873.7 32.9 %copy-start.2 = (f32[3,1152]{1,0:T(4,128)S(1)}, f32[3,1152]{1,0:T(4,128)}, u32[]{:S(2)}) copy-start(f32[3,1152]{1,0:T(4,128)} %get-tuple-element.231) | copy-start | bytes 41476
  873.7 32.9 %copy-start.3 = (f32[3,1152]{1,0:T(4,128)S(1)}, f32[3,1152]{1,0:T(4,128)}, u32[]{:S(2)}) copy-start(f32[3,1152]{1,0:T(4,128)} %get-tuple-element.288) | copy-start | bytes 41476
  873.7 33.2 %copy-start.8 = (f32[3]{0:T(128)S(1)}, f32[3]{0:T(128)}, u32[]{:S(2)}) copy-start(f32[3]{0:T(128)} %copy-done.7) | copy-start | bytes 40
  873.7 644.5 %copy-start.4 = (bf16[3,1152]{1,0:T(4,128)(2,1)S(1)}, bf16[3,1152]{1,0:T(4,128)(2,1)}, u32[]{:S(2)}) copy-start(bf16[3,1152]{1,0:T(4,128)(2,1)} %param.14) | copy-start | bytes 20740
  873.7 644.5 %copy-start.6 = (f32[3]{0:T(128)S(1)}, f32[3]{0:T(128)}, u32[]{:S(2)}) copy-start(f32[3]{0:T(128)} %copy-done.5) | copy-start | bytes 40
  875.0 28.7 %collective-permute-start.2 = (f32[192,1152]{1,0:T(8,128)S(1)}, f32[192,1152]{1,0:T(8,128)S(1)}, u32[]{:S(2)}, u32[]{:S(2)}) collective-permute-start(f32[192,1152]{1,0:T(8,128)S(1)} %convolution_add_fusion.2), channel_id=1, source_target_pairs={{0,64},{64,128},{128,192},{192,256},{256,320},{320,384},{384,448},... | collective-permute-start | bytes 2654216 | tf_op jit(solution)/shard_map/ppermute | solution.py:16
  903.7 0.9 copy-start.1
Sparse Core Ops, SparseCore 0:
  10.1 310.5 all-gather.7
  322.7 303.2 all-gather.5
  904.8 613.3 all-reduce.2
where the time goes:
time: 1530 us
  waiting for transfers between devices  1160 us (76%)
  blocking collectives  166 us (11%)
  starting transfers between devices  104 us (7%)
  matrix products  51.1 us (3%)
  local copies, waits for them, and re-layouts  22.4 us (1%)
  between operations  15.8 us (1%)
    unnamed x4, waiting for transfers between devices  612 us
    all_gather x1, waiting for transfers between devices, body(): lax.all_gather(value_weight, 'grp', axis=0, tiled=True)  289 us
    all_gather x1, blocking collectives, body(): group_block = lax.all_gather(text_low, 'grp', axis=0, tiled=True)  166 us
    all_gather x1, waiting for transfers between devices, body(): lax.all_gather(key_weight, 'grp', axis=0, tiled=True)  141 us
    ppermute x15, waiting for transfers between devices, from_behind(): lax.ppermute(shard, axis, [(i, (i + by) % peers) for i in range(peers)])  119 us
    ppermute x15, starting transfers between devices, from_behind(): lax.ppermute(shard, axis, [(i, (i + by) % peers) for i in range(peers)])  104 us
  transfers between devices with their start and end apart: 18, of which 11 were waited for; matrix products, arithmetic and copies ran while one was open for 2% of the time, Pallas kernels for 0%

commit v1 on v0

v1 whole, which is shorter than its diff:
```python
import math

import jax
import jax.numpy as jnp
from jax import lax
from jax.experimental import pallas as pl
from jax.experimental.pallas import tpu as pltpu
from jax.sharding import Mesh
from jax.sharding import PartitionSpec as P

D = 1152
TILES = D // 128
HEADS = 16
HEAD_DIM = 72
IMG_DEV = 3
PAIRS = 1536
EPS = 1e-06
ID_BASE = 64
ROWS = 768
LOW = -1e30

FINE = ("yh", "core", "yl", "x", "z")
FINE_SHAPE = (4, 2, 2, 4, 8)
SIDE = ("core", "yl", "x")
FAR = ("yh", "z")
GRP = ("yl", "x", "z")
N_SIDE = 16
N_FAR = 32
N_GRP = 64
W_ROWS = 18

AT_FOLDED = HEAD_DIM
AT_KEY = AT_FOLDED + HEADS
KEY_FIRST = 128 - AT_KEY
KEY_REST = HEAD_DIM - KEY_FIRST

TOPS = 2
AT_TOP = IMG_DEV
AT_TEXT = AT_TOP + TOPS * IMG_DEV
AT_ID = AT_TEXT + IMG_DEV
AT_SCALAR = AT_ID + 1
N_LANES = 8

f32 = jnp.float32
bf16 = jnp.bfloat16
VMEM = pl.BlockSpec(memory_space=pltpu.VMEM)
SMEM = pl.BlockSpec(memory_space=pltpu.SMEM)


def call(kernel, outs, scratch=(), **cost):
    many = len(outs) > 1
    return pl.pallas_call(
        kernel,
        out_shape=tuple(outs) if many else outs[0],
        out_specs=(VMEM,) * len(outs) if many else VMEM,
        scratch_shapes=list(scratch),
        compiler_params=pltpu.CompilerParams(vmem_limit_bytes=40 * 1024 * 1024),
        **cost,
    )


def shape(*dims, dtype=f32):
    return jax.ShapeDtypeStruct(dims, dtype)


def iota(dims, axis):
    return lax.broadcasted_iota(jnp.int32, dims, axis)


def dot_nt(a, b):
    return lax.dot_general(a, b, (((1,), (1,)), ((), ())), preferred_element_type=f32)


def dot(a, b):
    return jnp.dot(a, b, preferred_element_type=f32)


def exchange(blocks, axes):
    return lax.all_to_all(blocks, axes, 0, 0)


def weight_kernel(core_ref, key_ref, value_ref, query_ref, out_ref, tile):
    keys = key_ref[...].astype(f32)
    values = value_ref[...].astype(f32)
    products = keys * query_ref[...].astype(f32)
    high = products.astype(bf16)
    low = (products - high.astype(f32)).astype(bf16)
    members = jnp.where(iota((HEADS, D), 1) // HEAD_DIM == iota((HEADS, D), 0), 1.0, 0.0).astype(bf16)
    folded = (dot_nt(high, members) + dot_nt(low, members)) * (1.0 / math.sqrt(HEAD_DIM))
    mine = core_ref[0] == 0
    half = HEADS // 2 * HEAD_DIM
    keys = jnp.where(mine, keys[:, :half], keys[:, half:])
    values = jnp.where(mine, values[:, :half], values[:, half:])
    tile[...] = jnp.zeros_like(tile)
    for head in range(HEADS // 2):
        at = head * HEAD_DIM
        tile[:W_ROWS, :HEAD_DIM] = values[:, at : at + HEAD_DIM]
        tile[:W_ROWS, AT_FOLDED:AT_KEY] = folded
        tile[:W_ROWS, AT_KEY:] = keys[:, at : at + KEY_FIRST]
        for part in range(3):
            tile[W_ROWS:, part * KEY_REST : (part + 1) * KEY_REST] = keys[
                part * 6 : part * 6 + 6, at + KEY_FIRST : at + HEAD_DIM
            ]
        out_ref[head * 8 : head * 8 + 8] = jnp.broadcast_to(tile[...].astype(bf16)[None], (8, 24, 128))


def three_parts(value):
    first = value.astype(bf16).astype(f32)
    rest = value - first
    second = rest.astype(bf16).astype(f32)
    return first, second, rest - second


def context_kernel(weights_ref, patches_ref, segments_ref, tail_ref, out_ref, pair_ref, main, extra, rows, marks):
    for source in range(N_GRP):
        block = weights_ref[source].astype(f32)
        at = source * W_ROWS
        main[at : at + W_ROWS, :] = block[:W_ROWS]
        for part in range(3):
            extra[at + part * 6 : at + part * 6 + 6, :] = block[
                W_ROWS:, part * KEY_REST : (part + 1) * KEY_REST
            ]
    packed = main[...]
    pair_ref[...] = jnp.concatenate([packed, packed[:, AT_KEY:], extra[...]], axis=1).astype(bf16)
    scores = dot(patches_ref[...], packed.astype(bf16)).T[AT_FOLDED:AT_KEY]

    place = iota((HEADS, ROWS), 1)
    lanes = iota((HEADS, 128), 1)
    marks[...] = jnp.zeros_like(marks)
    rows[...] = jnp.zeros_like(rows)
    scalars = jnp.zeros((HEADS, 128), f32)

    def put(row, value):
        for tile in range(ROWS // 128):
            rows[tile, pl.ds(row, HEADS, stride=16), :] = value[:, tile * 128 : (tile + 1) * 128]

    for slot in range(IMG_DEV):
        masked = jnp.where(segments_ref[...] == slot, scores, LOW)
        peak = jnp.max(masked, axis=1, keepdims=True)
        powers = jnp.where(masked > 0.5 * LOW, jnp.exp(masked - peak), 0.0)
        total = jnp.sum(powers, axis=1, keepdims=True)
        best = peak
        values = []
        for top in range(TOPS):
            if top > 0:
                best = jnp.max(masked, axis=1, keepdims=True)
            there = best > 0.5 * LOW
            first = jnp.min(jnp.where(masked == best, place, ROWS), axis=1, keepdims=True)
            hit = (place == first) & there
            put(AT_TOP + slot * TOPS + top, jnp.where(hit, 1.0, 0.0))
            masked = jnp.where(hit, LOW, masked)
            powers = jnp.where(hit, 0.0, powers)
            values.append(jnp.where(there, 1.0, 0.0))
        others = powers / total
        put(slot, others)
        values = [
            *three_parts(peak + jnp.log(total)),
            *three_parts(jnp.sum(others, axis=1, keepdims=True)),
            *values,
        ]
        for index, value in enumerate(values):
            scalars = jnp.where(lanes == slot * N_LANES + index, value, scalars)
    marks[pl.ds(AT_SCALAR, HEADS, stride=16), :] = scalars
    picks = jnp.concatenate([rows[tile].astype(bf16) for tile in range(ROWS // 128)], axis=1)
    context = dot(picks, patches_ref[...])
    context = context.reshape(HEADS, 16, D) + tail_ref[...].astype(f32)[None]
    out_ref[:, :, 128:] = context[:, :, 128:].astype(bf16)
    out_ref[:, :, :128] = (context[:, :, :128] + marks[...].reshape(HEADS, 16, 128)).astype(bf16)


def project_kernel(near_ref, pair_ref, query_ref, out_ref, value_rows, key_rows):
    near = near_ref[...].reshape(N_SIDE * 16, D)
    both = dot(near, pair_ref[...])
    value_rows[...] = both[:, :128]
    key_rows[:, :HEAD_DIM] = both[:, 128:]
    pick = jnp.where(iota((N_SIDE, N_SIDE * 16), 1) == iota((N_SIDE, N_SIDE * 16), 0) * 16 + AT_SCALAR, 1.0, 0.0)
    scalars = dot(pick.astype(bf16), near[:, :128])
    query = query_ref[...]
    pooled = []
    for slot in range(IMG_DEV):
        at = slot * N_LANES
        level = scalars[:, at : at + 1] + scalars[:, at + 1 : at + 2] + scalars[:, at + 2 : at + 3]
        others = scalars[:, at + 3 : at + 4] + scalars[:, at + 4 : at + 5] + scalars[:, at + 5 : at + 6]
        some = others > 0.0
        peak = jnp.where(some, 0.0, LOW)
        powers, values = [], []
        for top in range(TOPS):
            at_row = pl.ds(AT_TOP + slot * TOPS + top, N_SIDE, stride=16)
            keys = key_rows[at_row, :][:, :HEAD_DIM].astype(bf16).astype(f32)
            score = jnp.sum(keys * query, axis=1, keepdims=True) / math.sqrt(HEAD_DIM)
            there = scalars[:, at + 6 + top : at + 7 + top] > 0.5
            score = jnp.where(there, score - level, LOW)
            peak = jnp.maximum(peak, score)
            powers.append((there, score))
            values.append(value_rows[at_row, :][:, :HEAD_DIM].astype(bf16).astype(f32))
        powers = [jnp.where(there, jnp.exp(score - peak), 0.0) for there, score in powers]
        shift = jnp.where(some, jnp.exp(jnp.where(some, -peak, 0.0)), 0.0)
        total = others * shift
        for power in powers:
            total = total + power
        result = value_rows[pl.ds(slot, N_SIDE, stride=16), :][:, :HEAD_DIM] * (shift / total)
        for power, value in zip(powers, values):
            result = result + (power / total).astype(bf16).astype(f32) * value
        pooled.append(result)
    out_ref[...] = jnp.broadcast_to(jnp.concatenate(pooled, axis=1)[None], out_ref.shape)


def unit_kernel(side_ref, pooled_ref, tail_ref, out_ref, low_ref, unit_ref, norm_ref, units, norms, block):
    side = side_ref[0]
    for slot in range(IMG_DEV):
        for head in range(HEADS):
            units[slot, :, head * HEAD_DIM : (head + 1) * HEAD_DIM] = pooled_ref[
                head, :, slot * HEAD_DIM : (slot + 1) * HEAD_DIM
            ]
    block[...] = tail_ref[...].astype(f32)
    for slot in range(IMG_DEV):
        pooled = units[slot]
        norm = jnp.sqrt(jnp.sum(pooled * pooled, axis=1, keepdims=True) + EPS)
        unit = pooled / norm
        units[slot] = unit
        norms[slot] = jnp.broadcast_to(norm, (N_SIDE, 128))
        low_ref[slot * N_SIDE : (slot + 1) * N_SIDE, :] = unit.astype(bf16)
        own = units[slot, pl.ds(side, 1), :]
        block[slot : slot + 1, :] = own
        unit_ref[slot : slot + 1, :] = own
        norm_ref[slot : slot + 1, :] = norms[slot, pl.ds(side, 1), :]
    out_ref[...] = jnp.broadcast_to(block[...].astype(bf16)[None], out_ref.shape)


def pair_kernel(params_ref, side_ref, far_ref, text_ref, low_ref, index_ref, out_ref):
    scale, offset = params_ref[0], params_ref[1]
    side = side_ref[0]
    far = far_ref[...].reshape(N_FAR * 8, D)
    near = jnp.concatenate([text_ref[...], low_ref[...]], axis=0)
    digit = iota((8, 128), 1)
    slot = iota((8, 128), 0)
    code = jnp.where(digit == slot, float(ID_BASE), 0.0) + jnp.where(digit == slot + IMG_DEV, 1.0, 0.0)
    code = jnp.where(slot < IMG_DEV, code, 0.0).astype(bf16)
    ids = dot_nt(code, far[:, :128])
    columns = N_FAR * 8
    column = iota((1, columns), 1)
    kind = column % 8
    device = column // 8
    index = ((device // 8) * N_SIDE + side) * 8 + device % 8
    index = index * IMG_DEV + kind - IMG_DEV
    for position in range(IMG_DEV):
        moved = pltpu.roll(ids, columns - (6 - position), 1)[position : position + 1]
        index = jnp.where(kind == position, moved.astype(jnp.int32), index)
    logits = scale * dot_nt(near, far) + offset
    pair_sign = jnp.where(index_ref[...] == index, 1.0, -1.0)
    scaled = scale * (-pair_sign * jax.nn.sigmoid(-pair_sign * logits) / PAIRS)
    wanted = iota((6 * N_SIDE, columns), 0) // (IMG_DEV * N_SIDE)
    scaled = jnp.where(kind // IMG_DEV == wanted, scaled, 0.0).astype(bf16)
    parts = dot(scaled, far)
    for tile in range(TILES):
        for row in range(6):
            out_ref[:, tile * 6 + row, :] = parts[
                row * N_SIDE : (row + 1) * N_SIDE, tile * 128 : (tile + 1) * 128
            ]


def final_kernel(parts_ref, unit_text_ref, text_norm_ref, unit_image_ref, image_norm_ref, image_ref, text_ref, sums):
    total = parts_ref[0]
    for source in range(1, N_SIDE):
        total = total + parts_ref[source]
    sums[...] = total
    whole = jnp.concatenate([sums[tile * 6 : tile * 6 + 6, :] for tile in range(TILES)], axis=1)
    for first, unit_ref, norm, out_ref in (
        (0, unit_text_ref, text_norm_ref[...], text_ref),
        (IMG_DEV, unit_image_ref, image_norm_ref[:, :1], image_ref),
    ):
        part = whole[first : first + IMG_DEV]
        unit = unit_ref[...]
        out_ref[...] = (part - unit * jnp.sum(unit * part, axis=1, keepdims=True)) / norm


def code_ids(ids):
    row = jnp.concatenate([ids // ID_BASE, ids % ID_BASE]).astype(bf16)
    return jnp.pad(row, (0, D - 2 * IMG_DEV))[None]


def read_ids(row):
    row = row.astype(jnp.int32)
    return row[:, :IMG_DEV] * ID_BASE + row[:, IMG_DEV : 2 * IMG_DEV]


def weight_messages(core, key_weight, value_weight, pool_query):
    return call(
        weight_kernel, [shape(N_GRP, 24, 128, dtype=bf16)], [pltpu.VMEM((24, 128), f32)],
        in_specs=[SMEM, VMEM, VMEM, VMEM],
    )(core, key_weight, value_weight, pool_query[None])


def context_messages(weights, patches, segments, tail):
    return call(
        context_kernel,
        [shape(HEADS, 16, D, dtype=bf16), shape(D, 128 + HEAD_DIM, dtype=bf16)],
        [
            pltpu.VMEM((D, 128), f32),
            pltpu.VMEM((D, KEY_REST), f32),
            pltpu.VMEM((ROWS // 128, HEADS * 16, 128), f32),
            pltpu.VMEM((HEADS * 16, 128), f32),
        ],
        in_specs=[VMEM] * 4,
    )(weights, patches, segments, tail)


def pooled_messages(near, pair, query):
    return call(
        project_kernel,
        [shape(N_SIDE, N_SIDE, IMG_DEV * HEAD_DIM)],
        [pltpu.VMEM((N_SIDE * 16, 128), f32), pltpu.VMEM((N_SIDE * 16, 128), f32)],
        in_specs=[VMEM] * 3,
    )(near, pair, query)


def unit_messages(side, pooled, tail):
    return call(
        unit_kernel,
        [
            shape(N_FAR, 8, D, dtype=bf16),
            shape(IMG_DEV * N_SIDE, D, dtype=bf16),
            shape(IMG_DEV, D),
            shape(IMG_DEV, 128),
        ],
        [pltpu.VMEM((IMG_DEV, N_SIDE, D), f32), pltpu.VMEM((IMG_DEV, N_SIDE, 128), f32), pltpu.VMEM((8, D), f32)],
        in_specs=[SMEM, VMEM, VMEM],
    )(side, pooled, tail)


def pair_messages(params, side, far, texts, lows, index):
    return call(
        pair_kernel, [shape(N_SIDE, 6 * TILES, 128)], in_specs=[SMEM, SMEM, VMEM, VMEM, VMEM, VMEM]
    )(params, side, far, texts, lows, index)


def gradients(parts, unit_text, text_norm, unit_image, image_norm):
    return call(
        final_kernel,
        [shape(IMG_DEV, D), shape(IMG_DEV, D)],
        [pltpu.VMEM((6 * TILES, 128), f32)],
        in_specs=[VMEM] * 5,
    )(parts, unit_text, text_norm, unit_image, image_norm)


def body(
    patches,
    segment_ids,
    image_ids,
    text_embeds,
    key_weight,
    value_weight,
    pool_query,
    logit_scale,
    logit_bias,
):
    yh, core, yl, x, z = (lax.axis_index(name) for name in FINE)
    side = (core * 2 + yl) * 4 + x
    weights = exchange(weight_messages(core[None], key_weight, value_weight, pool_query), GRP)

    text_full = text_embeds.astype(f32)
    text_norm = jnp.sqrt(jnp.sum(text_full * text_full, axis=1, keepdims=True) + EPS)
    unit_text = text_full / text_norm
    text_low = unit_text.astype(bf16)
    id_row = code_ids(image_ids)
    tail = jnp.concatenate(
        [jnp.zeros((AT_TEXT, D), bf16), text_low, id_row, jnp.zeros((16 - AT_SCALAR, D), bf16)], axis=0
    )
    query = lax.dynamic_slice_in_dim(pool_query, side * HEAD_DIM, HEAD_DIM)[None].astype(f32)
    context, pair = context_messages(weights, patches, segment_ids, tail)
    near = exchange(context, SIDE)
    pooled = exchange(pooled_messages(near, pair, query), SIDE)

    tail = jnp.concatenate(
        [jnp.zeros((IMG_DEV, D), bf16), text_low, id_row, jnp.zeros((1, D), bf16)], axis=0
    )
    far, lows, unit_image, image_norm = unit_messages(side[None], pooled, tail)
    far = exchange(far, FAR)

    texts = jnp.transpose(near[:, AT_TEXT:AT_ID], (1, 0, 2)).reshape(IMG_DEV * N_SIDE, D)
    side_dev = (yh * N_SIDE + jnp.arange(N_SIDE, dtype=jnp.int32)) * 8 + z
    text_index = side_dev[None, :] * IMG_DEV + jnp.arange(IMG_DEV, dtype=jnp.int32)[:, None]
    image_index = read_ids(near[:, AT_ID]).T
    index = jnp.concatenate([text_index, image_index], axis=0).reshape(6 * N_SIDE, 1)
    params = jnp.concatenate([logit_scale, logit_bias])
    parts = exchange(pair_messages(params, side[None], far, texts, lows, index), SIDE)
    return gradients(parts, unit_text, text_norm, unit_image, image_norm)


def solution(mesh):
    fine = Mesh(mesh.devices.reshape(FINE_SHAPE), FINE)
    rows = P(FINE, None)
    in_specs = (rows, rows, P(FINE), rows, P(GRP, None), P(GRP, None), P(), P(), P())
    return jax.shard_map(
        body, mesh=fine, in_specs=in_specs, out_specs=(rows, rows), check_vma=False
    )
```

time: 1530 us -> 117 us (0.08)
  the two profiles are of different devices: /device:TPU:56 before, /device:TPU:1 now
where the time goes in v1:
time: 117 us; the launch traced here: 116 us
  waiting for transfers between devices  58.8 us (50%)
  starting transfers between devices  36.6 us (31%)
  Pallas kernels  10.4 us (9%)
  local copies, waits for them, and re-layouts  4.95 us (4%)
  other arithmetic  3.71 us (3%)
  between operations  2.02 us (2%)
    all_to_all x5, waiting for transfers between devices, exchange(): return lax.all_to_all(blocks, axes, 0, 0)  58.8 us
    all_to_all x5, starting transfers between devices, exchange(): return lax.all_to_all(blocks, axes, 0, 0)  36.6 us
    unnamed x9, local copies, waits for them, and re-layouts  3.79 us
    pallas_call x1, Pallas kernels, context_messages(): call(context_kernel, [shape(HEADS, 16, D, dtype=bf16), shape(D, 128 + HEA...  3.63 us
  transfers between devices with their start and end apart: 5, of which 5 were waited for; matrix products, arithmetic and copies ran while one was open for 4% of the time, Pallas kernels for 0%

profile of v1, /device:TPU:1, one launch (start us, length us, event | category | flops | bytes accessed | tf_op | source)
XLA Modules:
  0.0 116.5 jit_solution(17682313539114163875)
XLA Ops:
  0.6 0.7 broadcast_in_dim.25.query_ref
  1.3 0.0 copy-start.1
  1.3 0.8 copy-done.1
  2.1 0.0 copy-start.2
  2.1 0.8 copy-done.2
  3.0 1.1 shard_map.104
  4.0 15.3 %all-to-all-start = ((bf16[64,24,128]{2,1,0:T(8,128)(2,1)}), bf16[64,24,128]{2,1,0:T(8,128)(2,1)S(1)}, u32[]{:S(2)}, u32[]{:S(2)}) async-start(bf16[64,24,128]{2,1,0:T(8,128)(2,1)} %shard_map.104), calls=%async_computation | async-start | bytes 786432 | tf_op jit(solution)/shard_map/all_to_all | solution.py:79
  19.4 0.8 fusion
  20.2 0.7 fusion.6
  20.9 0.1 fusion.4
  21.0 0.8 fusion.8
  21.8 0.1 pad_maximum_fusion.tail_ref
  21.9 12.3 %all-to-all-done.weights_ref = bf16[64,24,128]{2,1,0:T(8,128)(2,1)S(1)} async-done(((bf16[64,24,128]{2,1,0:T(8,128)(2,1)}), bf16[64,24,128]{2,1,0:T(8,128)(2,1)S(1)}, u32[]{:S(2)}, u32[]{:S(2)}) %all-to-all-start) | async-done | bytes 393248 | tf_op jit(solution)/shard_map/all_to_all | solution.py:79
  34.1 0.0 copy-start
  34.1 1.5 %copy-done = bf16[768,1152]{1,0:T(8,128)(2,1)S(1)} copy-done((bf16[768,1152]{1,0:T(8,128)(2,1)S(1)}, bf16[768,1152]{1,0:T(8,128)(2,1)}, u32[]{:S(2)}) %copy-start) | copy-done | bytes 1769496
  35.6 0.0 copy-start.3
  35.6 0.7 copy-done.3
  36.3 3.6 %shard_map.105 = (bf16[16,16,1152]{2,1,0:T(8,128)(2,1)}, bf16[1152,200]{1,0:T(8,128)(2,1)S(1)}) custom-call(bf16[64,24,128]{2,1,0:T(8,128)(2,1)S(1)} %all-to-all-done.weights_ref, bf16[768,1152]{1,0:T(8,128)(2,1)S(1)} %copy-done, s32[1,768]{1,0:T(1,128)S(1)} %copy-done.3, bf16[16,1152]{1,0:T(8,128)(2,1)S(1)} %pad_maximum_fusion.tail_ref), custom_call_target="tpu_custom_call" | custom-call | tf_op jit(solution)/shard_map/pallas_call | solution.py:295
  39.9 5.9 %all-to-all-start.1 = ((bf16[16,16,1152]{2,1,0:T(8,128)(2,1)}), bf16[16,16,1152]{2,1,0:T(8,128)(2,1)S(1)}, u32[]{:S(2)}, u32[]{:S(2)}) async-start(bf16[16,16,1152]{2,1,0:T(8,128)(2,1)} %get-tuple-element.8), calls=%async_computation.1 | async-start | bytes 1179648 | tf_op jit(solution)/shard_map/all_to_all | solution.py:79
  47.1 0.1 pad.10.clone
  47.2 0.8 bitcast_convert_fusion.query_ref
  47.9 0.1 pad_maximum_fusion.1.params_ref
  48.0 0.1 iota_add_fusion
  48.1 9.0 %all-to-all-done.1.near_ref = bf16[16,16,1152]{2,1,0:T(8,128)(2,1)S(1)} async-done(((bf16[16,16,1152]{2,1,0:T(8,128)(2,1)}), bf16[16,16,1152]{2,1,0:T(8,128)(2,1)S(1)}, u32[]{:S(2)}, u32[]{:S(2)}) %all-to-all-start.1) | async-done | bytes 589856 | tf_op jit(solution)/shard_map/all_to_all | solution.py:79
  57.1 1.7 %shard_map.106 = f32[16,16,216]{2,1,0:T(8,128)} custom-call(bf16[16,16,1152]{2,1,0:T(8,128)(2,1)S(1)} %all-to-all-done.1.near_ref, bf16[1152,200]{1,0:T(8,128)(2,1)S(1)} %get-tuple-element.9.pair_ref, f32[1,72]{1,0:T(1,128)S(1)} %bitcast_convert_fusion.query_ref), custom_call_target="tpu_custom_call" | custom-call | tf_op jit(solution)/shard_map/pallas_call | solution.py:309
  58.8 3.6 %all-to-all-start.2 = ((f32[16,16,216]{2,1,0:T(8,128)}), f32[16,16,216]{2,1,0:T(8,128)S(1)}, u32[]{:S(2)}, u32[]{:S(2)}) async-start(f32[16,16,216]{2,1,0:T(8,128)} %shard_map.106), calls=%async_computation.2 | async-start | bytes 524288 | tf_op jit(solution)/shard_map/all_to_all | solution.py:79
  62.4 0.1 maximum_maximum_fusion.tail_ref
  62.5 7.7 %all-to-all-done.2.pooled_ref = f32[16,16,216]{2,1,0:T(8,128)S(1)} async-done(((f32[16,16,216]{2,1,0:T(8,128)}), f32[16,16,216]{2,1,0:T(8,128)S(1)}, u32[]{:S(2)}, u32[]{:S(2)}) %all-to-all-start.2) | async-done | bytes 221216 | tf_op jit(solution)/shard_map/all_to_all | solution.py:79
  70.1 1.2 %shard_map.107 = (bf16[32,8,1152]{2,1,0:T(8,128)(2,1)}, bf16[48,1152]{1,0:T(8,128)(2,1)S(1)}, f32[3,1152]{1,0:T(4,128)S(1)}, f32[3,128]{1,0:T(4,128)S(1)}) custom-call(s32[1]{0:T(128)} %bitcast.side_ref, f32[16,16,216]{2,1,0:T(8,128)S(1)} %all-to-all-done.2.pooled_ref, bf16[8,1152]{1,0:T(8,128)(2,1)S(1)} %maximum_maximum_fusion.tail_ref), custom_call_target="tpu_custom_call" | custom-call | tf_op jit(solution)/shard_map/pallas_call | solution.py:318
  71.3 6.4 %all-to-all-start.3 = ((bf16[32,8,1152]{2,1,0:T(8,128)(2,1)}), bf16[32,8,1152]{2,1,0:T(8,128)(2,1)S(1)}, u32[]{:S(2)}, u32[]{:S(2)}) async-start(bf16[32,8,1152]{2,1,0:T(8,128)(2,1)} %get-tuple-element.10), calls=%async_computation.3 | async-start | bytes 1179648 | tf_op jit(solution)/shard_map/all_to_all | solution.py:79
  77.7 0.1 slice_bitcast_fusion
  77.8 0.1 slice_convert_fusion
  78.0 0.1 fusion.1
  78.1 0.1 pad_add_fusion
  78.1 0.1 copy.12
  78.2 0.1 reshape.41.index_ref
  78.3 20.1 %all-to-all-done.3.far_ref = bf16[32,8,1152]{2,1,0:T(8,128)(2,1)S(1)} async-done(((bf16[32,8,1152]{2,1,0:T(8,128)(2,1)}), bf16[32,8,1152]{2,1,0:T(8,128)(2,1)S(1)}, u32[]{:S(2)}, u32[]{:S(2)}) %all-to-all-start.3) | async-done | bytes 589856 | tf_op jit(solution)/shard_map/all_to_all | solution.py:79
  98.4 2.1 %shard_map.108 = f32[16,54,128]{2,1,0:T(8,128)} custom-call(f32[2]{0:T(128)S(1)} %pad_maximum_fusion.1.params_ref, s32[1]{0:T(128)} %bitcast.side_ref, bf16[32,8,1152]{2,1,0:T(8,128)(2,1)S(1)} %all-to-all-done.3.far_ref, bf16[48,1152]{1,0:T(8,128)(2,1)S(1)} %bitcast.16, bf16[48,1152]{1,0:T(8,128)(2,1)S(1)} %get-tuple-element.11.low_ref, ...), custom_call_target="tpu_custom_call" | custom-call | tf_op jit(solution)/shard_map/pallas_call | solution.py:332
  100.5 5.4 %all-to-all-start.4 = ((f32[16,54,128]{2,1,0:T(8,128)}), f32[16,54,128]{2,1,0:T(8,128)S(1)}, u32[]{:S(2)}, u32[]{:S(2)}) async-start(f32[16,54,128]{2,1,0:T(8,128)} %shard_map.108), calls=%async_computation.4 | async-start | bytes 917504 | tf_op jit(solution)/shard_map/all_to_all | solution.py:79
  105.9 0.1 copy.14.text_norm_ref
  106.0 9.8 %all-to-all-done.4.parts_ref = f32[16,54,128]{2,1,0:T(8,128)S(1)} async-done(((f32[16,54,128]{2,1,0:T(8,128)}), f32[16,54,128]{2,1,0:T(8,128)S(1)}, u32[]{:S(2)}, u32[]{:S(2)}) %all-to-all-start.4) | async-done | bytes 442400 | tf_op jit(solution)/shard_map/all_to_all | solution.py:79
  115.7 0.7 shard_map.109
  (8 shorter events, 0.1 us)
Async XLA Ops:
  1.3 0.8 copy-start.1
  2.1 0.8 copy-start.2
  4.0 30.1 %all-to-all-start = ((bf16[64,24,128]{2,1,0:T(8,128)(2,1)}), bf16[64,24,128]{2,1,0:T(8,128)(2,1)S(1)}, u32[]{:S(2)}, u32[]{:S(2)}) async-start(bf16[64,24,128]{2,1,0:T(8,128)(2,1)} %shard_map.104), calls=%async_computation | async-start | bytes 786432 | tf_op jit(solution)/shard_map/all_to_all | solution.py:79
  34.1 1.5 %copy-start = (bf16[768,1152]{1,0:T(8,128)(2,1)S(1)}, bf16[768,1152]{1,0:T(8,128)(2,1)}, u32[]{:S(2)}) copy-start(bf16[768,1152]{1,0:T(8,128)(2,1)} %patches_ref.1) | copy-start | bytes 5308420
  35.6 0.7 copy-start.3
  39.9 17.1 %all-to-all-start.1 = ((bf16[16,16,1152]{2,1,0:T(8,128)(2,1)}), bf16[16,16,1152]{2,1,0:T(8,128)(2,1)S(1)}, u32[]{:S(2)}, u32[]{:S(2)}) async-start(bf16[16,16,1152]{2,1,0:T(8,128)(2,1)} %get-tuple-element.8), calls=%async_computation.1 | async-start | bytes 1179648 | tf_op jit(solution)/shard_map/all_to_all | solution.py:79
  58.8 11.4 %all-to-all-start.2 = ((f32[16,16,216]{2,1,0:T(8,128)}), f32[16,16,216]{2,1,0:T(8,128)S(1)}, u32[]{:S(2)}, u32[]{:S(2)}) async-start(f32[16,16,216]{2,1,0:T(8,128)} %shard_map.106), calls=%async_computation.2 | async-start | bytes 524288 | tf_op jit(solution)/shard_map/all_to_all | solution.py:79
  71.3 27.1 %all-to-all-start.3 = ((bf16[32,8,1152]{2,1,0:T(8,128)(2,1)}), bf16[32,8,1152]{2,1,0:T(8,128)(2,1)S(1)}, u32[]{:S(2)}, u32[]{:S(2)}) async-start(bf16[32,8,1152]{2,1,0:T(8,128)(2,1)} %get-tuple-element.10), calls=%async_computation.3 | async-start | bytes 1179648 | tf_op jit(solution)/shard_map/all_to_all | solution.py:79
  100.5 15.2 %all-to-all-start.4 = ((f32[16,54,128]{2,1,0:T(8,128)}), f32[16,54,128]{2,1,0:T(8,128)S(1)}, u32[]{:S(2)}, u32[]{:S(2)}) async-start(f32[16,54,128]{2,1,0:T(8,128)} %shard_map.108), calls=%async_computation.4 | async-start | bytes 917504 | tf_op jit(solution)/shard_map/all_to_all | solution.py:79

commit v2 on v1

v2 whole, which is shorter than its diff:
```python
import math

import jax
import jax.numpy as jnp
from jax import lax
from jax.experimental import pallas as pl
from jax.experimental.pallas import tpu as pltpu
from jax.sharding import Mesh
from jax.sharding import PartitionSpec as P

D = 1152
TILES = D // 128
HEADS = 16
HEAD_DIM = 72
IMG_DEV = 3
PAIRS = 1536
EPS = 1e-06
ID_BASE = 64
ROWS = 768
LOW = -1e30

FINE = ("yh", "core", "yl", "x", "z")
FINE_SHAPE = (4, 2, 2, 4, 8)
SIDE = ("core", "yl", "x")
FAR = ("yh", "z")
GRP = ("yl", "x", "z")
N_SIDE = 16
N_FAR = 32
N_GRP = 64
W_ROWS = 18

AT_FOLDED = HEAD_DIM
AT_KEY = AT_FOLDED + HEADS
KEY_FIRST = 128 - AT_KEY
KEY_REST = HEAD_DIM - KEY_FIRST

TOPS = 2
AT_TOP = IMG_DEV
AT_TEXT = AT_TOP + TOPS * IMG_DEV
AT_ID = AT_TEXT + IMG_DEV
NEAR_LIST = AT_ID + 1
NEAR_ROWS = 120
AT_NEAR_ID = AT_ID
AT_SCALAR = NEAR_LIST + AT_ID
N_LANES = 8

AT_FAR_ID = 6 * TILES
FAR_ROWS = 56

f32 = jnp.float32
bf16 = jnp.bfloat16
VMEM = pl.BlockSpec(memory_space=pltpu.VMEM)
ANY = pl.BlockSpec(memory_space=pltpu.HBM)
SMEM = pl.BlockSpec(memory_space=pltpu.SMEM)


def call(kernel, outs, scratch=(), limit=40, **cost):
    many = len(outs) > 1
    return pl.pallas_call(
        kernel,
        out_shape=tuple(outs) if many else outs[0],
        out_specs=(VMEM,) * len(outs) if many else VMEM,
        scratch_shapes=list(scratch),
        compiler_params=pltpu.CompilerParams(vmem_limit_bytes=limit * 1024 * 1024),
        **cost,
    )


def shape(*dims, dtype=f32):
    return jax.ShapeDtypeStruct(dims, dtype)


def iota(dims, axis):
    return lax.broadcasted_iota(jnp.int32, dims, axis)


def dot_nt(a, b):
    return lax.dot_general(a, b, (((1,), (1,)), ((), ())), preferred_element_type=f32)


def dot(a, b):
    return jnp.dot(a, b, preferred_element_type=f32)


def exchange(blocks, axes):
    return lax.all_to_all(blocks, axes, 0, 0)


def weight_kernel(core_ref, key_hbm, value_hbm, query_hbm, out_ref, key_ref, value_ref, query_ref, tile, sems):
    copies = [
        pltpu.make_async_copy(source, target, sems.at[index])
        for index, (source, target) in enumerate(
            ((query_hbm, query_ref), (key_hbm, key_ref), (value_hbm, value_ref))
        )
    ]
    for copy in copies:
        copy.start()
    members = jnp.where(iota((HEADS, D), 1) // HEAD_DIM == iota((HEADS, D), 0), 1.0, 0.0).astype(bf16)
    tile[...] = jnp.zeros_like(tile)
    for copy in copies:
        copy.wait()
    keys = key_ref[...].astype(f32)
    values = value_ref[...].astype(f32)
    query = query_ref[...].astype(f32)
    query = jnp.concatenate([query[row : row + 1] for row in range(TILES)], axis=1)
    products = keys * query
    high = products.astype(bf16)
    low = (products - high.astype(f32)).astype(bf16)
    folded = (dot_nt(high, members) + dot_nt(low, members)) * (1.0 / math.sqrt(HEAD_DIM))
    mine = core_ref[0] == 0
    half = HEADS // 2 * HEAD_DIM
    keys = jnp.where(mine, keys[:, :half], keys[:, half:])
    values = jnp.where(mine, values[:, :half], values[:, half:])
    for head in range(HEADS // 2):
        at = head * HEAD_DIM
        tile[:W_ROWS, :HEAD_DIM] = values[:, at : at + HEAD_DIM]
        tile[:W_ROWS, AT_FOLDED:AT_KEY] = folded
        tile[:W_ROWS, AT_KEY:] = keys[:, at : at + KEY_FIRST]
        for part in range(3):
            tile[W_ROWS:, part * KEY_REST : (part + 1) * KEY_REST] = keys[
                part * 6 : part * 6 + 6, at + KEY_FIRST : at + HEAD_DIM
            ]
        out_ref[head * 8 : head * 8 + 8] = jnp.broadcast_to(tile[...].astype(bf16)[None], (8, 24, 128))


def three_parts(value):
    first = value.astype(bf16).astype(f32)
    rest = value - first
    second = rest.astype(bf16).astype(f32)
    return first, second, rest - second


def context_kernel(weights_ref, patches_ref, segments_ref, tail_ref, out_ref, main, sums):
    for source in range(N_GRP):
        at = source * W_ROWS
        main[at : at + W_ROWS, :] = weights_ref[source].astype(f32)[:W_ROWS]
    scores = dot(patches_ref[...], main[...].astype(bf16)).T[AT_FOLDED:AT_KEY]

    segments = segments_ref[...]
    masked = jnp.concatenate([jnp.where(segments == slot, scores, LOW) for slot in range(IMG_DEV)], axis=0)
    place = iota((IMG_DEV * HEADS, ROWS), 1)
    peak = jnp.max(masked, axis=1, keepdims=True)
    powers = jnp.where(masked > 0.5 * LOW, jnp.exp(masked - peak), 0.0)
    total = jnp.sum(powers, axis=1, keepdims=True)
    best = peak
    picks, values = [], []
    for top in range(TOPS):
        if top > 0:
            best = jnp.max(masked, axis=1, keepdims=True)
        there = best > 0.5 * LOW
        first = jnp.min(jnp.where(masked == best, place, ROWS), axis=1, keepdims=True)
        hit = (place == first) & there
        picks.append(jnp.where(hit, 1.0, 0.0).astype(bf16))
        masked = jnp.where(hit, LOW, masked)
        powers = jnp.where(hit, 0.0, powers)
        values.append(jnp.where(there, 1.0, 0.0))
    others = powers / total
    context = dot(jnp.concatenate([others.astype(bf16), *picks], axis=0), patches_ref[...])
    values = [
        *three_parts(peak + jnp.log(total)),
        *three_parts(jnp.sum(others, axis=1, keepdims=True)),
        *values,
    ]
    lanes = iota((IMG_DEV * HEADS, 128), 1) - iota((IMG_DEV * HEADS, 128), 0) // HEADS * N_LANES
    scalars = jnp.zeros((IMG_DEV * HEADS, 128), f32)
    for index, value in enumerate(values):
        scalars = jnp.where(lanes == index, value, scalars)
    scalars = scalars[:HEADS] + scalars[HEADS : 2 * HEADS] + scalars[2 * HEADS :]

    def put(row, value):
        sums[pl.ds(row, HEADS, stride=NEAR_ROWS), :] = value

    blank = jnp.zeros((HEADS, 128), f32)
    for tile in range(TILES):
        for row in range(AT_TEXT):
            put(tile * NEAR_LIST + row, context[row * HEADS : (row + 1) * HEADS, tile * 128 : (tile + 1) * 128])
        for row in range(AT_TEXT, NEAR_LIST):
            at = tile * NEAR_LIST + row
            put(at, scalars if at == AT_SCALAR else jnp.broadcast_to(tail_ref[at : at + 1, :], (HEADS, 128)))
    for row in range(TILES * NEAR_LIST, NEAR_ROWS):
        put(row, blank)
    out_ref[...] = sums[...].reshape(HEADS, NEAR_ROWS, 128).astype(bf16)


def project_kernel(place_ref, near_ref, weights_ref, query_ref, out_ref, text_ref, index_ref, rows, main, extra):
    for source in range(N_SIDE):
        rows[source * NEAR_ROWS : (source + 1) * NEAR_ROWS, :] = near_ref[source].astype(f32)
    for source in range(N_GRP):
        block = weights_ref[source].astype(f32)
        at = source * W_ROWS
        main[at : at + W_ROWS, :] = block[:W_ROWS]
        for part in range(3):
            extra[at + part * 6 : at + part * 6 + 6, :] = block[
                W_ROWS:, part * KEY_REST : (part + 1) * KEY_REST
            ]

    def take(row):
        return rows[pl.ds(row, N_SIDE, stride=NEAR_ROWS), :]

    near = jnp.concatenate(
        [
            jnp.concatenate([take(tile * NEAR_LIST + row) for row in range(AT_ID)], axis=0).astype(bf16)
            for tile in range(TILES)
        ],
        axis=1,
    )
    text_ref[...] = near[AT_TEXT * N_SIDE :]
    pair = jnp.concatenate([main[...], main[:, AT_KEY:], extra[...]], axis=1).astype(bf16)
    both = dot(near[: AT_TEXT * N_SIDE], pair)
    count = IMG_DEV * N_SIDE
    scalars = take(AT_SCALAR)
    lanes = iota((N_SIDE, 128), 1)

    def scalar(index):
        return jnp.concatenate(
            [
                jnp.sum(jnp.where(lanes == slot * N_LANES + index, scalars, 0.0), axis=1, keepdims=True)
                for slot in range(IMG_DEV)
            ],
            axis=0,
        )

    level = scalar(0) + scalar(1) + scalar(2)
    others = scalar(3) + scalar(4) + scalar(5)
    some = others > 0.0
    peak = jnp.where(some, 0.0, LOW)
    powers = []
    for top in range(TOPS):
        keys = both[(top + 1) * count : (top + 2) * count, 128:].astype(bf16).astype(f32)
        score = jnp.sum(keys * query_ref[...], axis=1, keepdims=True) / math.sqrt(HEAD_DIM)
        there = scalar(6 + top) > 0.5
        score = jnp.where(there, score - level, LOW)
        peak = jnp.maximum(peak, score)
        powers.append((there, score))
    powers = [jnp.where(there, jnp.exp(score - peak), 0.0) for there, score in powers]
    shift = jnp.where(some, jnp.exp(jnp.where(some, -peak, 0.0)), 0.0)
    total = others * shift
    for power in powers:
        total = total + power
    pooled = both[:count, :HEAD_DIM] * (shift / total)
    for top, power in enumerate(powers):
        value = both[(top + 1) * count : (top + 2) * count, :HEAD_DIM].astype(bf16).astype(f32)
        pooled = pooled + (power / total).astype(bf16).astype(f32) * value
    pooled = jnp.concatenate([pooled[slot * N_SIDE : (slot + 1) * N_SIDE] for slot in range(IMG_DEV)], axis=1)
    out_ref[...] = jnp.broadcast_to(pooled[None], out_ref.shape)

    ids = take(AT_NEAR_ID)
    member = iota((N_SIDE, 1), 0)
    for slot in range(IMG_DEV):
        text = ((place_ref[0] * N_SIDE + member) * 8 + place_ref[1]) * IMG_DEV + slot
        code = jnp.where(lanes == slot, float(ID_BASE), 0.0) + jnp.where(lanes == slot + IMG_DEV, 1.0, 0.0)
        image = jnp.sum(ids * code, axis=1, keepdims=True).astype(jnp.int32)
        index_ref[slot * N_SIDE : (slot + 1) * N_SIDE, :] = text
        index_ref[count + slot * N_SIDE : count + (slot + 1) * N_SIDE, :] = image


def unit_kernel(place_ref, pooled_ref, tail_ref, out_ref, low_ref, unit_ref, norm_ref, units, norms, block):
    side = place_ref[2]
    for slot in range(IMG_DEV):
        for head in range(HEADS):
            units[slot, :, head * HEAD_DIM : (head + 1) * HEAD_DIM] = pooled_ref[
                head, :, slot * HEAD_DIM : (slot + 1) * HEAD_DIM
            ]
    block[...] = tail_ref[...]

    def put(row, value):
        for tile in range(TILES):
            block[tile * 6 + row : tile * 6 + row + 1, :] = value[:, tile * 128 : (tile + 1) * 128]

    for slot in range(IMG_DEV):
        pooled = units[slot]
        norm = jnp.sqrt(jnp.sum(pooled * pooled, axis=1, keepdims=True) + EPS)
        unit = pooled / norm
        units[slot] = unit
        norms[slot] = jnp.broadcast_to(norm, (N_SIDE, 128))
        low_ref[slot * N_SIDE : (slot + 1) * N_SIDE, :] = unit.astype(bf16)
        own = units[slot, pl.ds(side, 1), :]
        put(slot, own)
        unit_ref[slot : slot + 1, :] = own
        norm_ref[slot : slot + 1, :] = norms[slot, pl.ds(side, 1), :]
    out_ref[...] = jnp.broadcast_to(block[...].astype(bf16)[None], out_ref.shape)


def pair_kernel(params_ref, place_ref, far_ref, text_ref, low_ref, index_ref, out_ref, far_rows, sums):
    scale, offset = params_ref[0], params_ref[1]
    for source in range(N_FAR):
        far_rows[source * FAR_ROWS : (source + 1) * FAR_ROWS, :] = far_ref[source].astype(f32)

    def take(row):
        return far_rows[pl.ds(row, N_FAR, stride=FAR_ROWS), :].astype(bf16)

    digit = iota((8, 128), 1)
    slot = iota((8, 128), 0)
    code = jnp.where(digit == slot, float(ID_BASE), 0.0) + jnp.where(digit == slot + IMG_DEV, 1.0, 0.0)
    ids = dot_nt(jnp.where(slot < IMG_DEV, code, 0.0).astype(bf16), take(AT_FAR_ID))
    ids = jnp.concatenate([ids[row : row + 1] for row in range(IMG_DEV)], axis=1).astype(jnp.int32)
    columns = IMG_DEV * N_FAR
    column = iota((1, columns), 1)
    device = column % N_FAR
    device = ((device // 8) * N_SIDE + place_ref[2]) * 8 + device % 8
    text_index = device * IMG_DEV + column // N_FAR
    sums[...] = jnp.zeros_like(sums)
    for first, near, index, place in ((0, text_ref[...], ids, 0), (IMG_DEV, low_ref[...], text_index, 1)):
        far = jnp.concatenate(
            [
                jnp.concatenate([take(tile * 6 + first + row) for row in range(IMG_DEV)], axis=0)
                for tile in range(TILES)
            ],
            axis=1,
        )
        logits = scale * dot_nt(near, far) + offset
        own = index_ref[place * IMG_DEV * N_SIDE : (place + 1) * IMG_DEV * N_SIDE, :]
        pair_sign = jnp.where(own == index, 1.0, -1.0)
        scaled = scale * (-pair_sign * jax.nn.sigmoid(-pair_sign * logits) / PAIRS)
        parts = dot(scaled.astype(bf16), far)
        for tile in range(TILES):
            for row in range(IMG_DEV):
                sums[pl.ds(tile * 6 + first + row, N_SIDE, stride=FAR_ROWS), :] = parts[
                    row * N_SIDE : (row + 1) * N_SIDE, tile * 128 : (tile + 1) * 128
                ]
    out_ref[...] = sums[...].reshape(N_SIDE, FAR_ROWS, 128).astype(bf16)


def final_kernel(parts_ref, unit_text_ref, text_norm_ref, unit_image_ref, image_norm_ref, image_ref, text_ref, sums):
    total = parts_ref[0].astype(f32)
    for source in range(1, N_SIDE):
        total = total + parts_ref[source].astype(f32)
    sums[...] = total
    whole = jnp.concatenate([sums[tile * 6 : tile * 6 + 6, :] for tile in range(TILES)], axis=1)
    for first, unit_ref, norm, out_ref in (
        (0, unit_text_ref, text_norm_ref[:, :1], text_ref),
        (IMG_DEV, unit_image_ref, image_norm_ref[:, :1], image_ref),
    ):
        part = whole[first : first + IMG_DEV]
        unit = unit_ref[...]
        out_ref[...] = (part - unit * jnp.sum(unit * part, axis=1, keepdims=True)) / norm


def tiled_rows(array):
    rows = array.shape[0]
    return jnp.transpose(array.reshape(rows, TILES, 128), (1, 0, 2))


def code_ids(ids):
    row = jnp.concatenate([ids // ID_BASE, ids % ID_BASE]).astype(f32)
    return jnp.pad(row, (0, 128 - 2 * IMG_DEV))[None]


def weight_messages(core, key_weight, value_weight, pool_query):
    return call(
        weight_kernel,
        [shape(N_GRP, 24, 128, dtype=bf16)],
        [
            pltpu.VMEM((W_ROWS, D), bf16),
            pltpu.VMEM((W_ROWS, D), bf16),
            pltpu.VMEM((TILES, 128), bf16),
            pltpu.VMEM((24, 128), f32),
            pltpu.SemaphoreType.DMA((3,)),
        ],
        limit=62,
        in_specs=[SMEM, ANY, ANY, ANY],
    )(core, key_weight, value_weight, pool_query.reshape(TILES, 128))


def fetch_kernel(patches_hbm, segments_hbm, patches_ref, segments_ref, sems):
    copies = [
        pltpu.make_async_copy(patches_hbm, patches_ref, sems.at[0]),
        pltpu.make_async_copy(segments_hbm, segments_ref, sems.at[1]),
    ]
    for copy in copies:
        copy.start()
    for copy in copies:
        copy.wait()


def fetch(patches, segments):
    return call(
        fetch_kernel,
        [shape(ROWS, D, dtype=bf16), shape(1, ROWS, dtype=jnp.int32)],
        [pltpu.SemaphoreType.DMA((2,))],
        in_specs=[ANY, ANY],
    )(patches, segments)


def context_messages(weights, patches, segments, tail):
    return call(
        context_kernel,
        [shape(HEADS, NEAR_ROWS, 128, dtype=bf16)],
        [pltpu.VMEM((D, 128), f32), pltpu.VMEM((HEADS * NEAR_ROWS, 128), f32)],
        in_specs=[VMEM] * 4,
    )(weights, patches, segments, tail)


def pooled_messages(place, near, weights, query):
    return call(
        project_kernel,
        [
            shape(N_SIDE, N_SIDE, IMG_DEV * HEAD_DIM),
            shape(IMG_DEV * N_SIDE, D, dtype=bf16),
            shape(2 * IMG_DEV * N_SIDE, 1, dtype=jnp.int32),
        ],
        [
            pltpu.VMEM((N_SIDE * NEAR_ROWS, 128), f32),
            pltpu.VMEM((D, 128), f32),
            pltpu.VMEM((D, KEY_REST), f32),
        ],
        in_specs=[SMEM] + [VMEM] * 3,
    )(place, near, weights, query)


def unit_messages(place, pooled, tail):
    return call(
        unit_kernel,
        [
            shape(N_FAR, FAR_ROWS, 128, dtype=bf16),
            shape(IMG_DEV * N_SIDE, D, dtype=bf16),
            shape(IMG_DEV, D),
            shape(IMG_DEV, 128),
        ],
        [pltpu.VMEM((IMG_DEV, N_SIDE, D), f32), pltpu.VMEM((IMG_DEV, N_SIDE, 128), f32), pltpu.VMEM((FAR_ROWS, 128), f32)],
        in_specs=[SMEM, VMEM, VMEM],
    )(place, pooled, tail)


def pair_messages(params, place, far, texts, lows, index):
    return call(
        pair_kernel,
        [shape(N_SIDE, FAR_ROWS, 128, dtype=bf16)],
        [pltpu.VMEM((N_FAR * FAR_ROWS, 128), f32), pltpu.VMEM((N_SIDE * FAR_ROWS, 128), f32)],
        in_specs=[SMEM, SMEM, VMEM, VMEM, VMEM, VMEM],
    )(params, place, far, texts, lows, index)


def gradients(parts, unit_text, text_norm, unit_image, image_norm):
    return call(
        final_kernel,
        [shape(IMG_DEV, D), shape(IMG_DEV, D)],
        [pltpu.VMEM((FAR_ROWS, 128), f32)],
        in_specs=[VMEM] * 5,
    )(parts, unit_text, text_norm, unit_image, image_norm)


def body(
    patches,
    segment_ids,
    image_ids,
    text_embeds,
    key_weight,
    value_weight,
    pool_query,
    logit_scale,
    logit_bias,
):
    yh, core, yl, x, z = (lax.axis_index(name) for name in FINE)
    side = (core * 2 + yl) * 4 + x
    weights = exchange(weight_messages(core[None], key_weight, value_weight, pool_query), GRP)

    text_full = text_embeds.astype(f32)
    text_norm = jnp.sqrt(jnp.sum(text_full * text_full, axis=1, keepdims=True) + EPS)
    unit_text = text_full / text_norm
    text_norm = jnp.broadcast_to(text_norm, (IMG_DEV, 128))
    text_low = tiled_rows(lax.reduce_precision(unit_text, 8, 7))
    ids = code_ids(image_ids)
    near_tail = jnp.pad(text_low, ((0, 0), (AT_TEXT, 1), (0, 0))).reshape(TILES * NEAR_LIST, 128)
    near_tail = jnp.where(jnp.arange(TILES * NEAR_LIST)[:, None] == AT_NEAR_ID, ids, near_tail)
    far_tail = jnp.pad(text_low, ((0, 0), (IMG_DEV, 0), (0, 0))).reshape(6 * TILES, 128)
    far_tail = jnp.concatenate([far_tail, ids, jnp.zeros((1, 128), f32)], axis=0)
    query = lax.dynamic_slice_in_dim(pool_query, side * HEAD_DIM, HEAD_DIM)[None].astype(f32)
    patches, segments = fetch(patches, segment_ids)
    params = jnp.concatenate([logit_scale, logit_bias])
    place = jnp.stack([yh, z, side])
    (weights, patches, segments, near_tail, far_tail, query, params, place, unit_text, text_norm) = (
        lax.optimization_barrier(
            (weights, patches, segments, near_tail, far_tail, query, params, place, unit_text, text_norm)
        )
    )

    near = exchange(context_messages(weights, patches, segments, near_tail), SIDE)
    pooled, texts, index = pooled_messages(place, near, weights, query)
    pooled = exchange(pooled, SIDE)
    far, lows, unit_image, image_norm = unit_messages(place, pooled, far_tail)
    far = exchange(far, FAR)
    parts = exchange(pair_messages(params, place, far, texts, lows, index), SIDE)
    return gradients(parts, unit_text, text_norm, unit_image, image_norm)


def solution(mesh):
    fine = Mesh(mesh.devices.reshape(FINE_SHAPE), FINE)
    rows = P(FINE, None)
    in_specs = (rows, rows, P(FINE), rows, P(GRP, None), P(GRP, None), P(), P(), P())
    return jax.shard_map(
        body, mesh=fine, in_specs=in_specs, out_specs=(rows, rows), check_vma=False
    )
```

time: 117 us -> 103 us (0.88)
  blocking collectives: 0 us -> 61.4 us
  waiting for transfers between devices: 58.8 us -> 8.18 us
  starting transfers between devices: 36.6 us -> 15.4 us
  local copies, waits for them, and re-layouts: 4.95 us -> 2.91 us
  Pallas kernels: 10.4 us -> 9.13 us
    all_to_all x0 -> x4, blocking collectives: none -> 61.4 us  [exchange(): return lax.all_to_all(blocks, axes, 0, 0)]
    all_to_all x5 -> x1, waiting for transfers between devices: 58.8 us -> 8.18 us  [exchange(): return lax.all_to_all(blocks, axes, 0, 0)]
    all_to_all x5 -> x1, starting transfers between devices: 36.6 us -> 15.4 us  [exchange(): return lax.all_to_all(blocks, axes, 0, 0)]
    pallas_call x6 -> x7, Pallas kernels: 10.4 us -> 9.13 us  [the longest x1 2.25 us: context_messages(): call(context_kernel, [shape(HEADS, NEAR_ROWS, 128, dtype=bf16)], [pltpu.V...]
  transfers between devices with their start and end apart: 5 -> 1, of which waited for: 5 -> 1; matrix products, arithmetic and copies ran while one was open for 4% -> 3% of each run, Pallas kernels for 0% -> 0%
where the time goes in v2:
time: 103 us; the launch traced here: 102 us
  blocking collectives  61.4 us (60%)
  starting transfers between devices  15.4 us (15%)
  Pallas kernels  9.13 us (9%)
  waiting for transfers between devices  8.18 us (8%)
  other arithmetic  3.43 us (3%)
  local copies, waits for them, and re-layouts  2.91 us (3%)
  between operations  2.08 us (2%)
    all_to_all x4, blocking collectives, exchange(): return lax.all_to_all(blocks, axes, 0, 0)  61.4 us
    all_to_all x1, starting transfers between devices, exchange(): return lax.all_to_all(blocks, axes, 0, 0)  15.4 us
    all_to_all x1, waiting for transfers between devices, exchange(): return lax.all_to_all(blocks, axes, 0, 0)  8.18 us
    unnamed x9, local copies, waits for them, and re-layouts  2.71 us
    pallas_call x1, Pallas kernels, context_messages(): call(context_kernel, [shape(HEADS, NEAR_ROWS, 128, dtype=bf16)], [pltpu.V...  2.25 us
    pallas_call x1, Pallas kernels, weight_messages(): call(weight_kernel, [shape(N_GRP, 24, 128, dtype=bf16)], [pltpu.VMEM((W_R...  2.1 us
  transfers between devices with their start and end apart: 1, of which 1 were waited for; matrix products, arithmetic and copies ran while one was open for 3% of the time, Pallas kernels for 0%

profile of v2, /device:TPU:1, one launch (start us, length us, event | category | flops | bytes accessed | tf_op | source)
XLA Modules:
  0.0 102.5 jit_solution(13080589380131619010)
XLA Ops:
  0.6 0.0 copy-start.3
  0.6 0.0 copy-start
  0.7 2.1 %shard_map.104 = bf16[64,24,128]{2,1,0:T(8,128)(2,1)} custom-call(s32[1]{0:T(128)} %bitcast.core_ref, bf16[18,1152]{1,0:T(8,128)(2,1)} %key_hbm.1, bf16[18,1152]{1,0:T(8,128)(2,1)} %value_hbm.1, bf16[9,128]{1,0:T(8,128)(2,1)} %bitcast.13), custom_call_target="tpu_custom_call" | custom-call | tf_op jit(solution)/shard_map/pallas_call | solution.py:350
  2.8 15.4 %all-to-all-start = ((bf16[64,24,128]{2,1,0:T(8,128)(2,1)}), bf16[64,24,128]{2,1,0:T(8,128)(2,1)S(1)}, u32[]{:S(2)}, u32[]{:S(2)}) async-start(bf16[64,24,128]{2,1,0:T(8,128)(2,1)} %shard_map.104), calls=%async_computation | async-start | bytes 786432 | tf_op jit(solution)/shard_map/all_to_all | solution.py:86
  18.2 0.8 fusion
  19.0 0.8 fusion.1
  21.2 0.8 bitcast_convert_fusion.query_ref
  21.9 0.7 and_select_fusion.1
  22.6 0.1 pad.22.clone
  22.7 0.1 add_convert_fusion
  22.8 0.0 copy-done.3
  22.8 0.0 copy-done
  22.8 0.4 shard_map.105
  23.1 0.0 copy-start.1
  23.2 1.2 %copy-done.1 = bf16[768,1152]{1,0:T(8,128)(2,1)} copy-done((bf16[768,1152]{1,0:T(8,128)(2,1)}, bf16[768,1152]{1,0:T(8,128)(2,1)S(1)}, u32[]{:S(2)}) %copy-start.1) | copy-done | bytes 1769496
  24.4 0.1 pad_maximum_fusion.params_ref
  24.5 0.1 pad_add_fusion.place_ref
  24.5 0.1 maximum_maximum_fusion.tail_ref
  24.6 0.1 broadcast_select_fusion.tail_ref
  24.7 8.2 %all-to-all-done.weights_ref = bf16[64,24,128]{2,1,0:T(8,128)(2,1)S(1)} async-done(((bf16[64,24,128]{2,1,0:T(8,128)(2,1)}), bf16[64,24,128]{2,1,0:T(8,128)(2,1)S(1)}, u32[]{:S(2)}, u32[]{:S(2)}) %all-to-all-start) | async-done | bytes 393248 | tf_op jit(solution)/shard_map/all_to_all | solution.py:86
  32.9 0.1 broadcast_in_dim.38.text_norm_ref
  32.9 0.0 copy-start.2
  33.0 1.5 %copy-done.2 = bf16[768,1152]{1,0:T(8,128)(2,1)S(1)} copy-done((bf16[768,1152]{1,0:T(8,128)(2,1)S(1)}, bf16[768,1152]{1,0:T(8,128)(2,1)}, u32[]{:S(2)}) %copy-start.2) | copy-done | bytes 1769496
  34.4 2.3 %shard_map.106 = bf16[16,120,128]{2,1,0:T(8,128)(2,1)S(1)} custom-call(bf16[64,24,128]{2,1,0:T(8,128)(2,1)S(1)} %all-to-all-done.weights_ref, bf16[768,1152]{1,0:T(8,128)(2,1)S(1)} %copy-done.2, s32[1,768]{1,0:T(1,128)S(1)} %get-tuple-element.27.segments_ref, f32[117,128]{1,0:T(8,128)S(1)} %broadcast_select_fusion.tail_ref), custom_call_target="tpu_custom_call" | custom-call | tf_op jit(solution)/shard_map/pallas_call | solution.py:386
  36.7 15.3 %all_to_all.25.near_ref = bf16[16,120,128]{2,1,0:T(8,128)(2,1)S(1)} all-to-all(bf16[16,120,128]{2,1,0:T(8,128)(2,1)S(1)} %shard_map.106), channel_id=1, replica_groups=mesh['yh'=4,'core'=2,'yl'=2,'x'=4,'z'=8] {'core','yl','x'}, dimensions={0} | all-to-all | bytes 983040 | tf_op jit(solution)/shard_map/all_to_all | solution.py:86
  52.0 1.4 %shard_map.107 = (f32[16,16,216]{2,1,0:T(8,128)S(1)}, bf16[48,1152]{1,0:T(8,128)(2,1)S(1)}, s32[96,1]{1,0:T(8,128)S(1)}) custom-call(s32[3]{0:T(128)S(1)} %pad_add_fusion.place_ref, bf16[16,120,128]{2,1,0:T(8,128)(2,1)S(1)} %all_to_all.25.near_ref, bf16[64,24,128]{2,1,0:T(8,128)(2,1)S(1)} %all-to-all-done.weights_ref, f32[1,72]{1,0:T(1,128)S(1)} %bitcast_convert_fusion.query_ref), custom_call_target="tpu_custom_call" | custom-call | tf_op jit(solution)/shard_map/pallas_call | solution.py:395
  53.4 10.7 %all_to_all.26.pooled_ref = f32[16,16,216]{2,1,0:T(8,128)S(1)} all-to-all(f32[16,16,216]{2,1,0:T(8,128)S(1)} %get-tuple-element.30), channel_id=1, replica_groups=mesh['yh'=4,'core'=2,'yl'=2,'x'=4,'z'=8] {'core','yl','x'}, dimensions={0} | all-to-all | bytes 442368 | tf_op jit(solution)/shard_map/all_to_all | solution.py:86
  64.1 0.9 shard_map.108
  65.0 24.0 %all_to_all.27.far_ref = bf16[32,56,128]{2,1,0:T(8,128)(2,1)S(1)} all-to-all(bf16[32,56,128]{2,1,0:T(8,128)(2,1)S(1)} %get-tuple-element.32), channel_id=1, replica_groups=mesh['yh'=4,'core'=2,'yl'=2,'x'=4,'z'=8] {'yh','z'}, dimensions={0} | all-to-all | bytes 917504 | tf_op jit(solution)/shard_map/all_to_all | solution.py:86
  89.0 1.4 %shard_map.109 = bf16[16,56,128]{2,1,0:T(8,128)(2,1)S(1)} custom-call(f32[2]{0:T(128)S(1)} %pad_maximum_fusion.params_ref, s32[3]{0:T(128)S(1)} %pad_add_fusion.place_ref, bf16[32,56,128]{2,1,0:T(8,128)(2,1)S(1)} %all_to_all.27.far_ref, bf16[48,1152]{1,0:T(8,128)(2,1)S(1)} %get-tuple-element.33.text_ref, bf16[48,1152]{1,0:T(8,128)(2,1)S(1)} %get-tuple-element.34.low_ref, ...), custom_call_target="tpu_custom_call" | custom-call | tf_op jit(solution)/shard_map/pallas_call | solution.py:426
  90.4 11.3 %all_to_all.28.parts_ref = bf16[16,56,128]{2,1,0:T(8,128)(2,1)S(1)} all-to-all(bf16[16,56,128]{2,1,0:T(8,128)(2,1)S(1)} %shard_map.109), channel_id=1, replica_groups=mesh['yh'=4,'core'=2,'yl'=2,'x'=4,'z'=8] {'core','yl','x'}, dimensions={0} | all-to-all | bytes 458752 | tf_op jit(solution)/shard_map/all_to_all | solution.py:86
  101.7 0.8 shard_map.110
  (9 shorter events, 0.1 us)
Async XLA Ops:
  0.6 22.1 %copy-start.3 = (s32[1,768]{1,0:T(1,128)S(1)}, s32[1,768]{1,0:T(1,128)}, u32[]{:S(2)}) copy-start(s32[1,768]{1,0:T(1,128)} %segments_hbm.1) | copy-start | bytes 9220
  0.6 22.1 %copy-start = (bf16[768,1152]{1,0:T(8,128)(2,1)S(1)}, bf16[768,1152]{1,0:T(8,128)(2,1)}, u32[]{:S(2)}) copy-start(bf16[768,1152]{1,0:T(8,128)(2,1)} %patches_hbm.1) | copy-start | bytes 5308420
  2.8 30.1 %all-to-all-start = ((bf16[64,24,128]{2,1,0:T(8,128)(2,1)}), bf16[64,24,128]{2,1,0:T(8,128)(2,1)S(1)}, u32[]{:S(2)}, u32[]{:S(2)}) async-start(bf16[64,24,128]{2,1,0:T(8,128)(2,1)} %shard_map.104), calls=%async_computation | async-start | bytes 786432 | tf_op jit(solution)/shard_map/all_to_all | solution.py:86
  23.1 1.2 %copy-start.1 = (bf16[768,1152]{1,0:T(8,128)(2,1)}, bf16[768,1152]{1,0:T(8,128)(2,1)S(1)}, u32[]{:S(2)}) copy-start(bf16[768,1152]{1,0:T(8,128)(2,1)S(1)} %get-tuple-element.26.patches_ref) | copy-start | bytes 5308420
  32.9 1.5 %copy-start.2 = (bf16[768,1152]{1,0:T(8,128)(2,1)S(1)}, bf16[768,1152]{1,0:T(8,128)(2,1)}, u32[]{:S(2)}) copy-start(bf16[768,1152]{1,0:T(8,128)(2,1)} %copy-done.1) | copy-start | bytes 5308420

commit v3 on v2

--- a/solution.py
+++ b/solution.py
@@ -469,10 +469,8 @@
     patches, segments = fetch(patches, segment_ids)
     params = jnp.concatenate([logit_scale, logit_bias])
     place = jnp.stack([yh, z, side])
-    (weights, patches, segments, near_tail, far_tail, query, params, place, unit_text, text_norm) = (
-        lax.optimization_barrier(
-            (weights, patches, segments, near_tail, far_tail, query, params, place, unit_text, text_norm)
-        )
+    weights, near_tail, far_tail, query, params, place, unit_text, text_norm = lax.optimization_barrier(
+        (weights, near_tail, far_tail, query, params, place, unit_text, text_norm)
     )
 
     near = exchange(context_messages(weights, patches, segments, near_tail), SIDE)

time: 103 us -> 103 us (level)
  no operation moved by 1% of the time
where the time goes in v3:
time: 103 us; the launch traced here: 102 us
  blocking collectives  61.4 us (60%)
  starting transfers between devices  15.4 us (15%)
  Pallas kernels  9.13 us (9%)
  waiting for transfers between devices  8.18 us (8%)
  other arithmetic  3.43 us (3%)
  local copies, waits for them, and re-layouts  2.91 us (3%)
  between operations  2.08 us (2%)
    all_to_all x4, blocking collectives, exchange(): return lax.all_to_all(blocks, axes, 0, 0)  61.4 us
    all_to_all x1, starting transfers between devices, exchange(): return lax.all_to_all(blocks, axes, 0, 0)  15.4 us
    all_to_all x1, waiting for transfers between devices, exchange(): return lax.all_to_all(blocks, axes, 0, 0)  8.18 us
    unnamed x9, local copies, waits for them, and re-layouts  2.71 us
    pallas_call x1, Pallas kernels, context_messages(): call(context_kernel, [shape(HEADS, NEAR_ROWS, 128, dtype=bf16)], [pltpu.V...  2.25 us
    pallas_call x1, Pallas kernels, weight_messages(): call(weight_kernel, [shape(N_GRP, 24, 128, dtype=bf16)], [pltpu.VMEM((W_R...  2.1 us
  transfers between devices with their start and end apart: 1, of which 1 were waited for; matrix products, arithmetic and copies ran while one was open for 3% of the time, Pallas kernels for 0%

profile of v3, /device:TPU:1, one launch (start us, length us, event | category | flops | bytes accessed | tf_op | source)
XLA Modules:
  0.0 102.5 jit_solution(13080589380131619010)
XLA Ops:
  0.6 0.0 copy-start.3
  0.6 0.0 copy-start
  0.7 2.1 %shard_map.104 = bf16[64,24,128]{2,1,0:T(8,128)(2,1)} custom-call(s32[1]{0:T(128)} %bitcast.core_ref, bf16[18,1152]{1,0:T(8,128)(2,1)} %key_hbm.1, bf16[18,1152]{1,0:T(8,128)(2,1)} %value_hbm.1, bf16[9,128]{1,0:T(8,128)(2,1)} %bitcast.13), custom_call_target="tpu_custom_call" | custom-call | tf_op jit(solution)/shard_map/pallas_call | solution.py:350
  2.8 15.4 %all-to-all-start = ((bf16[64,24,128]{2,1,0:T(8,128)(2,1)}), bf16[64,24,128]{2,1,0:T(8,128)(2,1)S(1)}, u32[]{:S(2)}, u32[]{:S(2)}) async-start(bf16[64,24,128]{2,1,0:T(8,128)(2,1)} %shard_map.104), calls=%async_computation | async-start | bytes 786432 | tf_op jit(solution)/shard_map/all_to_all | solution.py:86
  18.2 0.8 fusion
  19.0 0.8 fusion.1
  21.2 0.8 bitcast_convert_fusion.query_ref
  21.9 0.7 and_select_fusion.1
  22.6 0.1 pad.22.clone
  22.7 0.1 add_convert_fusion
  22.8 0.0 copy-done.3
  22.8 0.0 copy-done
  22.8 0.4 shard_map.105
  23.1 0.0 copy-start.1
  23.2 1.2 %copy-done.1 = bf16[768,1152]{1,0:T(8,128)(2,1)} copy-done((bf16[768,1152]{1,0:T(8,128)(2,1)}, bf16[768,1152]{1,0:T(8,128)(2,1)S(1)}, u32[]{:S(2)}) %copy-start.1) | copy-done | bytes 1769496
  24.4 0.1 pad_maximum_fusion.params_ref
  24.5 0.1 pad_add_fusion.place_ref
  24.5 0.1 maximum_maximum_fusion.tail_ref
  24.6 0.1 broadcast_select_fusion.tail_ref
  24.7 8.2 %all-to-all-done.weights_ref = bf16[64,24,128]{2,1,0:T(8,128)(2,1)S(1)} async-done(((bf16[64,24,128]{2,1,0:T(8,128)(2,1)}), bf16[64,24,128]{2,1,0:T(8,128)(2,1)S(1)}, u32[]{:S(2)}, u32[]{:S(2)}) %all-to-all-start) | async-done | bytes 393248 | tf_op jit(solution)/shard_map/all_to_all | solution.py:86
  32.9 0.1 broadcast_in_dim.38.text_norm_ref
  32.9 0.0 copy-start.2
  33.0 1.5 %copy-done.2 = bf16[768,1152]{1,0:T(8,128)(2,1)S(1)} copy-done((bf16[768,1152]{1,0:T(8,128)(2,1)S(1)}, bf16[768,1152]{1,0:T(8,128)(2,1)}, u32[]{:S(2)}) %copy-start.2) | copy-done | bytes 1769496
  34.4 2.3 %shard_map.106 = bf16[16,120,128]{2,1,0:T(8,128)(2,1)S(1)} custom-call(bf16[64,24,128]{2,1,0:T(8,128)(2,1)S(1)} %all-to-all-done.weights_ref, bf16[768,1152]{1,0:T(8,128)(2,1)S(1)} %copy-done.2, s32[1,768]{1,0:T(1,128)S(1)} %get-tuple-element.23.segments_ref, f32[117,128]{1,0:T(8,128)S(1)} %broadcast_select_fusion.tail_ref), custom_call_target="tpu_custom_call" | custom-call | tf_op jit(solution)/shard_map/pallas_call | solution.py:386
  36.7 15.3 %all_to_all.25.near_ref = bf16[16,120,128]{2,1,0:T(8,128)(2,1)S(1)} all-to-all(bf16[16,120,128]{2,1,0:T(8,128)(2,1)S(1)} %shard_map.106), channel_id=1, replica_groups=mesh['yh'=4,'core'=2,'yl'=2,'x'=4,'z'=8] {'core','yl','x'}, dimensions={0} | all-to-all | bytes 983040 | tf_op jit(solution)/shard_map/all_to_all | solution.py:86
  52.0 1.4 %shard_map.107 = (f32[16,16,216]{2,1,0:T(8,128)S(1)}, bf16[48,1152]{1,0:T(8,128)(2,1)S(1)}, s32[96,1]{1,0:T(8,128)S(1)}) custom-call(s32[3]{0:T(128)S(1)} %pad_add_fusion.place_ref, bf16[16,120,128]{2,1,0:T(8,128)(2,1)S(1)} %all_to_all.25.near_ref, bf16[64,24,128]{2,1,0:T(8,128)(2,1)S(1)} %all-to-all-done.weights_ref, f32[1,72]{1,0:T(1,128)S(1)} %bitcast_convert_fusion.query_ref), custom_call_target="tpu_custom_call" | custom-call | tf_op jit(solution)/shard_map/pallas_call | solution.py:395
  53.4 10.7 %all_to_all.26.pooled_ref = f32[16,16,216]{2,1,0:T(8,128)S(1)} all-to-all(f32[16,16,216]{2,1,0:T(8,128)S(1)} %get-tuple-element.26), channel_id=1, replica_groups=mesh['yh'=4,'core'=2,'yl'=2,'x'=4,'z'=8] {'core','yl','x'}, dimensions={0} | all-to-all | bytes 442368 | tf_op jit(solution)/shard_map/all_to_all | solution.py:86
  64.1 0.9 shard_map.108
  65.0 24.0 %all_to_all.27.far_ref = bf16[32,56,128]{2,1,0:T(8,128)(2,1)S(1)} all-to-all(bf16[32,56,128]{2,1,0:T(8,128)(2,1)S(1)} %get-tuple-element.28), channel_id=1, replica_groups=mesh['yh'=4,'core'=2,'yl'=2,'x'=4,'z'=8] {'yh','z'}, dimensions={0} | all-to-all | bytes 917504 | tf_op jit(solution)/shard_map/all_to_all | solution.py:86
  89.0 1.4 %shard_map.109 = bf16[16,56,128]{2,1,0:T(8,128)(2,1)S(1)} custom-call(f32[2]{0:T(128)S(1)} %pad_maximum_fusion.params_ref, s32[3]{0:T(128)S(1)} %pad_add_fusion.place_ref, bf16[32,56,128]{2,1,0:T(8,128)(2,1)S(1)} %all_to_all.27.far_ref, bf16[48,1152]{1,0:T(8,128)(2,1)S(1)} %get-tuple-element.29.text_ref, bf16[48,1152]{1,0:T(8,128)(2,1)S(1)} %get-tuple-element.30.low_ref, ...), custom_call_target="tpu_custom_call" | custom-call | tf_op jit(solution)/shard_map/pallas_call | solution.py:426
  90.4 11.3 %all_to_all.28.parts_ref = bf16[16,56,128]{2,1,0:T(8,128)(2,1)S(1)} all-to-all(bf16[16,56,128]{2,1,0:T(8,128)(2,1)S(1)} %shard_map.109), channel_id=1, replica_groups=mesh['yh'=4,'core'=2,'yl'=2,'x'=4,'z'=8] {'core','yl','x'}, dimensions={0} | all-to-all | bytes 458752 | tf_op jit(solution)/shard_map/all_to_all | solution.py:86
  101.7 0.8 shard_map.110
  (9 shorter events, 0.1 us)
Async XLA Ops:
  0.6 22.1 %copy-start.3 = (s32[1,768]{1,0:T(1,128)S(1)}, s32[1,768]{1,0:T(1,128)}, u32[]{:S(2)}) copy-start(s32[1,768]{1,0:T(1,128)} %segments_hbm.1) | copy-start | bytes 9220
  0.6 22.1 %copy-start = (bf16[768,1152]{1,0:T(8,128)(2,1)S(1)}, bf16[768,1152]{1,0:T(8,128)(2,1)}, u32[]{:S(2)}) copy-start(bf16[768,1152]{1,0:T(8,128)(2,1)} %patches_hbm.1) | copy-start | bytes 5308420
  2.8 30.1 %all-to-all-start = ((bf16[64,24,128]{2,1,0:T(8,128)(2,1)}), bf16[64,24,128]{2,1,0:T(8,128)(2,1)S(1)}, u32[]{:S(2)}, u32[]{:S(2)}) async-start(bf16[64,24,128]{2,1,0:T(8,128)(2,1)} %shard_map.104), calls=%async_computation | async-start | bytes 786432 | tf_op jit(solution)/shard_map/all_to_all | solution.py:86
  23.1 1.2 %copy-start.1 = (bf16[768,1152]{1,0:T(8,128)(2,1)}, bf16[768,1152]{1,0:T(8,128)(2,1)S(1)}, u32[]{:S(2)}) copy-start(bf16[768,1152]{1,0:T(8,128)(2,1)S(1)} %get-tuple-element.22.patches_ref) | copy-start | bytes 5308420
  32.9 1.5 %copy-start.2 = (bf16[768,1152]{1,0:T(8,128)(2,1)S(1)}, bf16[768,1152]{1,0:T(8,128)(2,1)}, u32[]{:S(2)}) copy-start(bf16[768,1152]{1,0:T(8,128)(2,1)} %copy-done.1) | copy-start | bytes 5308420

commit v4 on v3

--- a/solution.py
+++ b/solution.py
@@ -17,6 +17,7 @@
 EPS = 1e-06
 ID_BASE = 64
 ROWS = 768
+CHUNKS = 3
 LOW = -1e30
 
 FINE = ("yh", "core", "yl", "x", "z")
@@ -130,11 +131,28 @@
     return first, second, rest - second
 
 
-def context_kernel(weights_ref, patches_ref, segments_ref, tail_ref, out_ref, main, sums):
+def context_kernel(
+    weights_ref, patches_hbm, segments_hbm, tail_ref, out_ref, patches_ref, segments_ref, main, sums, sems
+):
+    step = ROWS // CHUNKS
+    spans = [pl.ds(chunk * step, step) for chunk in range(CHUNKS)]
+    copies = [
+        pltpu.make_async_copy(patches_hbm.at[span], patches_ref.at[span], sems.at[chunk])
+        for chunk, span in enumerate(spans)
+    ]
+    copies.append(pltpu.make_async_copy(segments_hbm, segments_ref, sems.at[CHUNKS]))
+    for copy in copies:
+        copy.start()
     for source in range(N_GRP):
         at = source * W_ROWS
         main[at : at + W_ROWS, :] = weights_ref[source].astype(f32)[:W_ROWS]
-    scores = dot(patches_ref[...], main[...].astype(bf16)).T[AT_FOLDED:AT_KEY]
+    folded = main[...].astype(bf16)
+    scores = []
+    for copy, span in zip(copies, spans):
+        copy.wait()
+        scores.append(dot(patches_ref[span, :], folded).T[AT_FOLDED:AT_KEY])
+    scores = jnp.concatenate(scores, axis=1)
+    copies[CHUNKS].wait()
 
     segments = segments_ref[...]
     masked = jnp.concatenate([jnp.where(segments == slot, scores, LOW) for slot in range(IMG_DEV)], axis=0)
@@ -362,32 +380,19 @@
     )(core, key_weight, value_weight, pool_query.reshape(TILES, 128))
 
 
-def fetch_kernel(patches_hbm, segments_hbm, patches_ref, segments_ref, sems):
-    copies = [
-        pltpu.make_async_copy(patches_hbm, patches_ref, sems.at[0]),
-        pltpu.make_async_copy(segments_hbm, segments_ref, sems.at[1]),
-    ]
-    for copy in copies:
-        copy.start()
-    for copy in copies:
-        copy.wait()
-
-
-def fetch(patches, segments):
-    return call(
-        fetch_kernel,
-        [shape(ROWS, D, dtype=bf16), shape(1, ROWS, dtype=jnp.int32)],
-        [pltpu.SemaphoreType.DMA((2,))],
-        in_specs=[ANY, ANY],
-    )(patches, segments)
-
-
 def context_messages(weights, patches, segments, tail):
     return call(
         context_kernel,
         [shape(HEADS, NEAR_ROWS, 128, dtype=bf16)],
-        [pltpu.VMEM((D, 128), f32), pltpu.VMEM((HEADS * NEAR_ROWS, 128), f32)],
-        in_specs=[VMEM] * 4,
+        [
+            pltpu.VMEM((ROWS, D), bf16),
+            pltpu.VMEM((1, ROWS), jnp.int32),
+            pltpu.VMEM((D, 128), f32),
+            pltpu.VMEM((HEADS * NEAR_ROWS, 128), f32),
+            pltpu.SemaphoreType.DMA((CHUNKS + 1,)),
+        ],
+        limit=52,
+        in_specs=[VMEM, ANY, ANY, VMEM],
     )(weights, patches, segments, tail)
 
 
@@ -466,14 +471,13 @@
     far_tail = jnp.pad(text_low, ((0, 0), (IMG_DEV, 0), (0, 0))).reshape(6 * TILES, 128)
     far_tail = jnp.concatenate([far_tail, ids, jnp.zeros((1, 128), f32)], axis=0)
     query = lax.dynamic_slice_in_dim(pool_query, side * HEAD_DIM, HEAD_DIM)[None].astype(f32)
-    patches, segments = fetch(patches, segment_ids)
     params = jnp.concatenate([logit_scale, logit_bias])
     place = jnp.stack([yh, z, side])
     weights, near_tail, far_tail, query, params, place, unit_text, text_norm = lax.optimization_barrier(
         (weights, near_tail, far_tail, query, params, place, unit_text, text_norm)
     )
 
-    near = exchange(context_messages(weights, patches, segments, near_tail), SIDE)
+    near = exchange(context_messages(weights, patches, segment_ids, near_tail), SIDE)
     pooled, texts, index = pooled_messages(place, near, weights, query)
     pooled = exchange(pooled, SIDE)
     far, lows, unit_image, image_norm = unit_messages(place, pooled, far_tail)

time: 103 us -> 102 us (level)
  local copies, waits for them, and re-layouts: 2.91 us -> 0.21 us
  waiting for transfers between devices: 8.18 us -> 9.8 us
    unnamed x9 -> x3, local copies, waits for them, and re-layouts: 2.71 us -> 0.01 us
    all_to_all x1, waiting for transfers between devices: 8.18 us -> 9.8 us  [exchange(): return lax.all_to_all(blocks, axes, 0, 0)]
    pallas_call x1, Pallas kernels: 2.25 us -> 3.29 us  [context_messages(): call(context_kernel, [shape(HEADS, NEAR_ROWS, 128, dtype=bf16)], [pltpu.V...]
  transfers between devices with their start and end apart: 1 -> 1, of which waited for: 1 -> 1; matrix products, arithmetic and copies ran while one was open for 3% -> 4% of each run, Pallas kernels for 0% -> 0%
where the time goes in v4:
time: 102 us
  blocking collectives  61.4 us (60%)
  starting transfers between devices  15.4 us (15%)
  waiting for transfers between devices  9.8 us (10%)
  Pallas kernels  9.64 us (9%)
  other arithmetic  3.44 us (3%)
  between operations  2.06 us (2%)
    all_to_all x4, blocking collectives, exchange(): return lax.all_to_all(blocks, axes, 0, 0)  61.4 us
    all_to_all x1, starting transfers between devices, exchange(): return lax.all_to_all(blocks, axes, 0, 0)  15.4 us
    all_to_all x1, waiting for transfers between devices, exchange(): return lax.all_to_all(blocks, axes, 0, 0)  9.8 us
    pallas_call x1, Pallas kernels, context_messages(): call(context_kernel, [shape(HEADS, NEAR_ROWS, 128, dtype=bf16)], [pltpu.V...  3.29 us
  transfers between devices with their start and end apart: 1, of which 1 were waited for; matrix products, arithmetic and copies ran while one was open for 4% of the time, Pallas kernels for 0%

profile of v4, /device:TPU:1, one launch (start us, length us, event | category | flops | bytes accessed | tf_op | source)
XLA Modules:
  0.0 101.9 jit_solution(16938643877734881587)
XLA Ops:
  0.6 0.0 copy-start
  0.6 2.0 %shard_map.104 = bf16[64,24,128]{2,1,0:T(8,128)(2,1)} custom-call(s32[1]{0:T(128)} %bitcast.core_ref, bf16[18,1152]{1,0:T(8,128)(2,1)} %key_hbm.1, bf16[18,1152]{1,0:T(8,128)(2,1)} %value_hbm.1, bf16[9,128]{1,0:T(8,128)(2,1)} %bitcast.13), custom_call_target="tpu_custom_call" | custom-call | tf_op jit(solution)/shard_map/pallas_call | solution.py:368
  2.6 15.4 %all-to-all-start = ((bf16[64,24,128]{2,1,0:T(8,128)(2,1)}), bf16[64,24,128]{2,1,0:T(8,128)(2,1)S(1)}, u32[]{:S(2)}, u32[]{:S(2)}) async-start(bf16[64,24,128]{2,1,0:T(8,128)(2,1)} %shard_map.104), calls=%async_computation | async-start | bytes 786432 | tf_op jit(solution)/shard_map/all_to_all | solution.py:87
  18.0 0.8 fusion
  18.8 0.8 fusion.1
  21.0 0.8 bitcast_convert_fusion.query_ref
  21.8 0.7 and_select_fusion.1
  22.4 0.1 pad.22.clone
  22.5 0.1 add_convert_fusion
  22.6 0.1 pad_maximum_fusion.params_ref
  22.7 0.1 pad_add_fusion.place_ref
  22.7 0.1 maximum_maximum_fusion.tail_ref
  22.8 0.1 broadcast_select_fusion.tail_ref
  22.9 9.8 %all-to-all-done.weights_ref = bf16[64,24,128]{2,1,0:T(8,128)(2,1)S(1)} async-done(((bf16[64,24,128]{2,1,0:T(8,128)(2,1)}), bf16[64,24,128]{2,1,0:T(8,128)(2,1)S(1)}, u32[]{:S(2)}, u32[]{:S(2)}) %all-to-all-start) | async-done | bytes 393248 | tf_op jit(solution)/shard_map/all_to_all | solution.py:87
  32.7 0.1 broadcast_in_dim.38.text_norm_ref
  32.8 0.0 copy-done
  32.8 3.3 %shard_map.105 = bf16[16,120,128]{2,1,0:T(8,128)(2,1)S(1)} custom-call(bf16[64,24,128]{2,1,0:T(8,128)(2,1)S(1)} %all-to-all-done.weights_ref, bf16[768,1152]{1,0:T(8,128)(2,1)} %patches_hbm.1, s32[1,768]{1,0:T(1,128)S(1)} %copy-done, f32[117,128]{1,0:T(8,128)S(1)} %broadcast_select_fusion.tail_ref), custom_call_target="tpu_custom_call" | custom-call | tf_op jit(solution)/shard_map/pallas_call | solution.py:384
  36.1 15.3 %all_to_all.25.near_ref = bf16[16,120,128]{2,1,0:T(8,128)(2,1)S(1)} all-to-all(bf16[16,120,128]{2,1,0:T(8,128)(2,1)S(1)} %shard_map.105), channel_id=1, replica_groups=mesh['yh'=4,'core'=2,'yl'=2,'x'=4,'z'=8] {'core','yl','x'}, dimensions={0} | all-to-all | bytes 983040 | tf_op jit(solution)/shard_map/all_to_all | solution.py:87
  51.4 1.4 %shard_map.106 = (f32[16,16,216]{2,1,0:T(8,128)S(1)}, bf16[48,1152]{1,0:T(8,128)(2,1)S(1)}, s32[96,1]{1,0:T(8,128)S(1)}) custom-call(s32[3]{0:T(128)S(1)} %pad_add_fusion.place_ref, bf16[16,120,128]{2,1,0:T(8,128)(2,1)S(1)} %all_to_all.25.near_ref, bf16[64,24,128]{2,1,0:T(8,128)(2,1)S(1)} %all-to-all-done.weights_ref, f32[1,72]{1,0:T(1,128)S(1)} %bitcast_convert_fusion.query_ref), custom_call_target="tpu_custom_call" | custom-call | tf_op jit(solution)/shard_map/pallas_call | solution.py:400
  52.8 10.7 %all_to_all.26.pooled_ref = f32[16,16,216]{2,1,0:T(8,128)S(1)} all-to-all(f32[16,16,216]{2,1,0:T(8,128)S(1)} %get-tuple-element.22), channel_id=1, replica_groups=mesh['yh'=4,'core'=2,'yl'=2,'x'=4,'z'=8] {'core','yl','x'}, dimensions={0} | all-to-all | bytes 442368 | tf_op jit(solution)/shard_map/all_to_all | solution.py:87
  63.5 0.9 shard_map.107
  64.4 24.1 %all_to_all.27.far_ref = bf16[32,56,128]{2,1,0:T(8,128)(2,1)S(1)} all-to-all(bf16[32,56,128]{2,1,0:T(8,128)(2,1)S(1)} %get-tuple-element.24), channel_id=1, replica_groups=mesh['yh'=4,'core'=2,'yl'=2,'x'=4,'z'=8] {'yh','z'}, dimensions={0} | all-to-all | bytes 917504 | tf_op jit(solution)/shard_map/all_to_all | solution.py:87
  88.4 1.4 %shard_map.108 = bf16[16,56,128]{2,1,0:T(8,128)(2,1)S(1)} custom-call(f32[2]{0:T(128)S(1)} %pad_maximum_fusion.params_ref, s32[3]{0:T(128)S(1)} %pad_add_fusion.place_ref, bf16[32,56,128]{2,1,0:T(8,128)(2,1)S(1)} %all_to_all.27.far_ref, bf16[48,1152]{1,0:T(8,128)(2,1)S(1)} %get-tuple-element.25.text_ref, bf16[48,1152]{1,0:T(8,128)(2,1)S(1)} %get-tuple-element.26.low_ref, ...), custom_call_target="tpu_custom_call" | custom-call | tf_op jit(solution)/shard_map/pallas_call | solution.py:431
  89.8 11.3 %all_to_all.28.parts_ref = bf16[16,56,128]{2,1,0:T(8,128)(2,1)S(1)} all-to-all(bf16[16,56,128]{2,1,0:T(8,128)(2,1)S(1)} %shard_map.108), channel_id=1, replica_groups=mesh['yh'=4,'core'=2,'yl'=2,'x'=4,'z'=8] {'core','yl','x'}, dimensions={0} | all-to-all | bytes 458752 | tf_op jit(solution)/shard_map/all_to_all | solution.py:87
  101.1 0.8 shard_map.109
  (9 shorter events, 0.1 us)
Async XLA Ops:
  0.6 32.2 %copy-start = (s32[1,768]{1,0:T(1,128)S(1)}, s32[1,768]{1,0:T(1,128)}, u32[]{:S(2)}) copy-start(s32[1,768]{1,0:T(1,128)} %segments_hbm.1) | copy-start | bytes 9220
  2.6 30.1 %all-to-all-start = ((bf16[64,24,128]{2,1,0:T(8,128)(2,1)}), bf16[64,24,128]{2,1,0:T(8,128)(2,1)S(1)}, u32[]{:S(2)}, u32[]{:S(2)}) async-start(bf16[64,24,128]{2,1,0:T(8,128)(2,1)} %shard_map.104), calls=%async_computation | async-start | bytes 786432 | tf_op jit(solution)/shard_map/all_to_all | solution.py:87

commit v5 on v3

--- a/solution.py
+++ b/solution.py
@@ -378,6 +378,7 @@
         fetch_kernel,
         [shape(ROWS, D, dtype=bf16), shape(1, ROWS, dtype=jnp.int32)],
         [pltpu.SemaphoreType.DMA((2,))],
+        limit=51,
         in_specs=[ANY, ANY],
     )(patches, segments)
 

time: 103 us -> 101 us (0.981)
  local copies, waits for them, and re-layouts: 2.91 us -> 0.21 us
    unnamed x9 -> x3, local copies, waits for them, and re-layouts: 2.71 us -> 0.01 us
    pallas_call x1, Pallas kernels: 0.38 us -> 1.5 us  [fetch(): call(fetch_kernel, [shape(ROWS, D, dtype=bf16), shape(1, ROWS, dtype=jnp....]
  transfers between devices with their start and end apart: 1 -> 1, of which waited for: 1 -> 1; matrix products, arithmetic and copies ran while one was open for 3% -> 4% of each run, Pallas kernels for 0% -> 1%
where the time goes in v5:
time: 101 us
  blocking collectives  61.4 us (61%)
  starting transfers between devices  15.4 us (15%)
  Pallas kernels  10.1 us (10%)
  waiting for transfers between devices  8.28 us (8%)
  other arithmetic  3.44 us (3%)
  between operations  2.07 us (2%)
    all_to_all x4, blocking collectives, exchange(): return lax.all_to_all(blocks, axes, 0, 0)  61.4 us
    all_to_all x1, starting transfers between devices, exchange(): return lax.all_to_all(blocks, axes, 0, 0)  15.4 us
    all_to_all x1, waiting for transfers between devices, exchange(): return lax.all_to_all(blocks, axes, 0, 0)  8.28 us
    pallas_call x1, Pallas kernels, context_messages(): call(context_kernel, [shape(HEADS, NEAR_ROWS, 128, dtype=bf16)], [pltpu.V...  2.25 us
  transfers between devices with their start and end apart: 1, of which 1 were waited for; matrix products, arithmetic and copies ran while one was open for 4% of the time, Pallas kernels for 1%

profile of v5, /device:TPU:1, one launch (start us, length us, event | category | flops | bytes accessed | tf_op | source)
XLA Modules:
  0.0 100.8 jit_solution(10813926416026513362)
XLA Ops:
  0.6 0.0 copy-start
  0.6 2.0 %shard_map.104 = bf16[64,24,128]{2,1,0:T(8,128)(2,1)} custom-call(s32[1]{0:T(128)} %bitcast.core_ref, bf16[18,1152]{1,0:T(8,128)(2,1)} %key_hbm.1, bf16[18,1152]{1,0:T(8,128)(2,1)} %value_hbm.1, bf16[9,128]{1,0:T(8,128)(2,1)} %bitcast.13), custom_call_target="tpu_custom_call" | custom-call | tf_op jit(solution)/shard_map/pallas_call | solution.py:350
  2.6 15.4 %all-to-all-start = ((bf16[64,24,128]{2,1,0:T(8,128)(2,1)}), bf16[64,24,128]{2,1,0:T(8,128)(2,1)S(1)}, u32[]{:S(2)}, u32[]{:S(2)}) async-start(bf16[64,24,128]{2,1,0:T(8,128)(2,1)} %shard_map.104), calls=%async_computation | async-start | bytes 786432 | tf_op jit(solution)/shard_map/all_to_all | solution.py:86
  18.0 0.8 fusion
  18.8 0.8 fusion.1
  21.0 0.8 bitcast_convert_fusion.query_ref
  21.8 0.7 and_select_fusion.1
  22.5 0.1 pad.22.clone
  22.5 0.1 add_convert_fusion
  22.6 0.0 copy-done
  22.6 1.5 %shard_map.105 = (bf16[768,1152]{1,0:T(8,128)(2,1)S(1)}, s32[1,768]{1,0:T(1,128)S(1)}) custom-call(bf16[768,1152]{1,0:T(8,128)(2,1)} %patches_hbm.1, s32[1,768]{1,0:T(1,128)S(1)} %copy-done), custom_call_target="tpu_custom_call" | custom-call | tf_op jit(solution)/shard_map/pallas_call | solution.py:377
  24.1 0.1 pad_maximum_fusion.params_ref
  24.2 0.1 pad_add_fusion.place_ref
  24.3 0.1 maximum_maximum_fusion.tail_ref
  24.4 0.1 broadcast_select_fusion.tail_ref
  24.4 8.3 %all-to-all-done.weights_ref = bf16[64,24,128]{2,1,0:T(8,128)(2,1)S(1)} async-done(((bf16[64,24,128]{2,1,0:T(8,128)(2,1)}), bf16[64,24,128]{2,1,0:T(8,128)(2,1)S(1)}, u32[]{:S(2)}, u32[]{:S(2)}) %all-to-all-start) | async-done | bytes 393248 | tf_op jit(solution)/shard_map/all_to_all | solution.py:86
  32.7 0.1 broadcast_in_dim.38.text_norm_ref
  32.8 2.3 %shard_map.106 = bf16[16,120,128]{2,1,0:T(8,128)(2,1)S(1)} custom-call(bf16[64,24,128]{2,1,0:T(8,128)(2,1)S(1)} %all-to-all-done.weights_ref, bf16[768,1152]{1,0:T(8,128)(2,1)S(1)} %get-tuple-element.22.patches_ref, s32[1,768]{1,0:T(1,128)S(1)} %get-tuple-element.23.segments_ref, f32[117,128]{1,0:T(8,128)S(1)} %broadcast_select_fusion.tail_ref), custom_call_target="tpu_custom_call" | custom-call | tf_op jit(solution)/shard_map/pallas_call | solution.py:387
  35.1 15.3 %all_to_all.25.near_ref = bf16[16,120,128]{2,1,0:T(8,128)(2,1)S(1)} all-to-all(bf16[16,120,128]{2,1,0:T(8,128)(2,1)S(1)} %shard_map.106), channel_id=1, replica_groups=mesh['yh'=4,'core'=2,'yl'=2,'x'=4,'z'=8] {'core','yl','x'}, dimensions={0} | all-to-all | bytes 983040 | tf_op jit(solution)/shard_map/all_to_all | solution.py:86
  50.4 1.4 %shard_map.107 = (f32[16,16,216]{2,1,0:T(8,128)S(1)}, bf16[48,1152]{1,0:T(8,128)(2,1)S(1)}, s32[96,1]{1,0:T(8,128)S(1)}) custom-call(s32[3]{0:T(128)S(1)} %pad_add_fusion.place_ref, bf16[16,120,128]{2,1,0:T(8,128)(2,1)S(1)} %all_to_all.25.near_ref, bf16[64,24,128]{2,1,0:T(8,128)(2,1)S(1)} %all-to-all-done.weights_ref, f32[1,72]{1,0:T(1,128)S(1)} %bitcast_convert_fusion.query_ref), custom_call_target="tpu_custom_call" | custom-call | tf_op jit(solution)/shard_map/pallas_call | solution.py:396
  51.7 10.7 %all_to_all.26.pooled_ref = f32[16,16,216]{2,1,0:T(8,128)S(1)} all-to-all(f32[16,16,216]{2,1,0:T(8,128)S(1)} %get-tuple-element.26), channel_id=1, replica_groups=mesh['yh'=4,'core'=2,'yl'=2,'x'=4,'z'=8] {'core','yl','x'}, dimensions={0} | all-to-all | bytes 442368 | tf_op jit(solution)/shard_map/all_to_all | solution.py:86
  62.4 0.9 shard_map.108
  63.3 24.1 %all_to_all.27.far_ref = bf16[32,56,128]{2,1,0:T(8,128)(2,1)S(1)} all-to-all(bf16[32,56,128]{2,1,0:T(8,128)(2,1)S(1)} %get-tuple-element.28), channel_id=1, replica_groups=mesh['yh'=4,'core'=2,'yl'=2,'x'=4,'z'=8] {'yh','z'}, dimensions={0} | all-to-all | bytes 917504 | tf_op jit(solution)/shard_map/all_to_all | solution.py:86
  87.4 1.4 %shard_map.109 = bf16[16,56,128]{2,1,0:T(8,128)(2,1)S(1)} custom-call(f32[2]{0:T(128)S(1)} %pad_maximum_fusion.params_ref, s32[3]{0:T(128)S(1)} %pad_add_fusion.place_ref, bf16[32,56,128]{2,1,0:T(8,128)(2,1)S(1)} %all_to_all.27.far_ref, bf16[48,1152]{1,0:T(8,128)(2,1)S(1)} %get-tuple-element.29.text_ref, bf16[48,1152]{1,0:T(8,128)(2,1)S(1)} %get-tuple-element.30.low_ref, ...), custom_call_target="tpu_custom_call" | custom-call | tf_op jit(solution)/shard_map/pallas_call | solution.py:427
  88.8 11.3 %all_to_all.28.parts_ref = bf16[16,56,128]{2,1,0:T(8,128)(2,1)S(1)} all-to-all(bf16[16,56,128]{2,1,0:T(8,128)(2,1)S(1)} %shard_map.109), channel_id=1, replica_groups=mesh['yh'=4,'core'=2,'yl'=2,'x'=4,'z'=8] {'core','yl','x'}, dimensions={0} | all-to-all | bytes 458752 | tf_op jit(solution)/shard_map/all_to_all | solution.py:86
  100.1 0.8 shard_map.110
  (9 shorter events, 0.1 us)
Async XLA Ops:
  0.6 22.0 %copy-start = (s32[1,768]{1,0:T(1,128)S(1)}, s32[1,768]{1,0:T(1,128)}, u32[]{:S(2)}) copy-start(s32[1,768]{1,0:T(1,128)} %segments_hbm.1) | copy-start | bytes 9220
  2.6 30.1 %all-to-all-start = ((bf16[64,24,128]{2,1,0:T(8,128)(2,1)}), bf16[64,24,128]{2,1,0:T(8,128)(2,1)S(1)}, u32[]{:S(2)}, u32[]{:S(2)}) async-start(bf16[64,24,128]{2,1,0:T(8,128)(2,1)} %shard_map.104), calls=%async_computation | async-start | bytes 786432 | tf_op jit(solution)/shard_map/all_to_all | solution.py:86

commit v6 on v5

--- a/solution.py
+++ b/solution.py
@@ -134,7 +134,7 @@
     for source in range(N_GRP):
         at = source * W_ROWS
         main[at : at + W_ROWS, :] = weights_ref[source].astype(f32)[:W_ROWS]
-    scores = dot(patches_ref[...], main[...].astype(bf16)).T[AT_FOLDED:AT_KEY]
+    scores = dot_nt(main[...].T[AT_FOLDED:AT_KEY].astype(bf16), patches_ref[...])
 
     segments = segments_ref[...]
     masked = jnp.concatenate([jnp.where(segments == slot, scores, LOW) for slot in range(IMG_DEV)], axis=0)
@@ -242,7 +242,7 @@
         value = both[(top + 1) * count : (top + 2) * count, :HEAD_DIM].astype(bf16).astype(f32)
         pooled = pooled + (power / total).astype(bf16).astype(f32) * value
     pooled = jnp.concatenate([pooled[slot * N_SIDE : (slot + 1) * N_SIDE] for slot in range(IMG_DEV)], axis=1)
-    out_ref[...] = jnp.broadcast_to(pooled[None], out_ref.shape)
+    out_ref[...] = jnp.broadcast_to(pooled.astype(bf16)[None], out_ref.shape)
 
     ids = take(AT_NEAR_ID)
     member = iota((N_SIDE, 1), 0)
@@ -256,10 +256,11 @@
 
 def unit_kernel(place_ref, pooled_ref, tail_ref, out_ref, low_ref, unit_ref, norm_ref, units, norms, block):
     side = place_ref[2]
-    for slot in range(IMG_DEV):
-        for head in range(HEADS):
-            units[slot, :, head * HEAD_DIM : (head + 1) * HEAD_DIM] = pooled_ref[
-                head, :, slot * HEAD_DIM : (slot + 1) * HEAD_DIM
+    for head in range(HEADS):
+        pooled = pooled_ref[head].astype(f32)
+        for slot in range(IMG_DEV):
+            units[slot, :, head * HEAD_DIM : (head + 1) * HEAD_DIM] = pooled[
+                :, slot * HEAD_DIM : (slot + 1) * HEAD_DIM
             ]
     block[...] = tail_ref[...]
 
@@ -396,7 +397,7 @@
     return call(
         project_kernel,
         [
-            shape(N_SIDE, N_SIDE, IMG_DEV * HEAD_DIM),
+            shape(N_SIDE, N_SIDE, IMG_DEV * HEAD_DIM, dtype=bf16),
             shape(IMG_DEV * N_SIDE, D, dtype=bf16),
             shape(2 * IMG_DEV * N_SIDE, 1, dtype=jnp.int32),
         ],

time: 101 us -> 99.5 us (0.985)
  blocking collectives: 61.4 us -> 59.8 us
    all_to_all x4, blocking collectives: 61.4 us -> 59.8 us  [exchange(): return lax.all_to_all(blocks, axes, 0, 0)]
  transfers between devices with their start and end apart: 1 -> 1, of which waited for: 1 -> 1; matrix products, arithmetic and copies ran while one was open for 4% -> 4% of each run, Pallas kernels for 1% -> 2%
where the time goes in v6:
time: 99.5 us; the launch traced here: 98.9 us
  blocking collectives  59.8 us (60%)
  starting transfers between devices  15.4 us (15%)
  Pallas kernels  9.73 us (10%)
  waiting for transfers between devices  8.28 us (8%)
  other arithmetic  3.44 us (3%)
  between operations  2.07 us (2%)
    all_to_all x4, blocking collectives, exchange(): return lax.all_to_all(blocks, axes, 0, 0)  59.8 us
    all_to_all x1, starting transfers between devices, exchange(): return lax.all_to_all(blocks, axes, 0, 0)  15.4 us
    all_to_all x1, waiting for transfers between devices, exchange(): return lax.all_to_all(blocks, axes, 0, 0)  8.28 us
  transfers between devices with their start and end apart: 1, of which 1 were waited for; matrix products, arithmetic and copies ran while one was open for 4% of the time, Pallas kernels for 2%

profile of v6, /device:TPU:1, one launch (start us, length us, event | category | flops | bytes accessed | tf_op | source)
XLA Modules:
  0.0 98.9 jit_solution(12465761585207900776)
XLA Ops:
  0.6 0.0 copy-start
  0.6 2.0 %shard_map.104 = bf16[64,24,128]{2,1,0:T(8,128)(2,1)} custom-call(s32[1]{0:T(128)} %bitcast.core_ref, bf16[18,1152]{1,0:T(8,128)(2,1)} %key_hbm.1, bf16[18,1152]{1,0:T(8,128)(2,1)} %value_hbm.1, bf16[9,128]{1,0:T(8,128)(2,1)} %bitcast.13), custom_call_target="tpu_custom_call" | custom-call | tf_op jit(solution)/shard_map/pallas_call | solution.py:351
  2.6 15.4 %all-to-all-start = ((bf16[64,24,128]{2,1,0:T(8,128)(2,1)}), bf16[64,24,128]{2,1,0:T(8,128)(2,1)S(1)}, u32[]{:S(2)}, u32[]{:S(2)}) async-start(bf16[64,24,128]{2,1,0:T(8,128)(2,1)} %shard_map.104), calls=%async_computation | async-start | bytes 786432 | tf_op jit(solution)/shard_map/all_to_all | solution.py:86
  18.0 0.8 fusion
  18.8 0.8 fusion.1
  21.0 0.8 bitcast_convert_fusion.query_ref
  21.8 0.7 and_select_fusion.1
  22.5 0.1 pad.22.clone
  22.5 0.1 add_convert_fusion
  22.6 0.0 copy-done
  22.6 1.5 %shard_map.105 = (bf16[768,1152]{1,0:T(8,128)(2,1)S(1)}, s32[1,768]{1,0:T(1,128)S(1)}) custom-call(bf16[768,1152]{1,0:T(8,128)(2,1)} %patches_hbm.1, s32[1,768]{1,0:T(1,128)S(1)} %copy-done), custom_call_target="tpu_custom_call" | custom-call | tf_op jit(solution)/shard_map/pallas_call | solution.py:378
  24.1 0.1 pad_maximum_fusion.params_ref
  24.2 0.1 pad_add_fusion.place_ref
  24.3 0.1 maximum_maximum_fusion.tail_ref
  24.4 0.1 broadcast_select_fusion.tail_ref
  24.4 8.3 %all-to-all-done.weights_ref = bf16[64,24,128]{2,1,0:T(8,128)(2,1)S(1)} async-done(((bf16[64,24,128]{2,1,0:T(8,128)(2,1)}), bf16[64,24,128]{2,1,0:T(8,128)(2,1)S(1)}, u32[]{:S(2)}, u32[]{:S(2)}) %all-to-all-start) | async-done | bytes 393248 | tf_op jit(solution)/shard_map/all_to_all | solution.py:86
  32.7 0.1 broadcast_in_dim.38.text_norm_ref
  32.8 1.9 %shard_map.106 = bf16[16,120,128]{2,1,0:T(8,128)(2,1)S(1)} custom-call(bf16[64,24,128]{2,1,0:T(8,128)(2,1)S(1)} %all-to-all-done.weights_ref, bf16[768,1152]{1,0:T(8,128)(2,1)S(1)} %get-tuple-element.22.patches_ref, s32[1,768]{1,0:T(1,128)S(1)} %get-tuple-element.23.segments_ref, f32[117,128]{1,0:T(8,128)S(1)} %broadcast_select_fusion.tail_ref), custom_call_target="tpu_custom_call" | custom-call | tf_op jit(solution)/shard_map/pallas_call | solution.py:388
  34.7 15.3 %all_to_all.25.near_ref = bf16[16,120,128]{2,1,0:T(8,128)(2,1)S(1)} all-to-all(bf16[16,120,128]{2,1,0:T(8,128)(2,1)S(1)} %shard_map.106), channel_id=1, replica_groups=mesh['yh'=4,'core'=2,'yl'=2,'x'=4,'z'=8] {'core','yl','x'}, dimensions={0} | all-to-all | bytes 983040 | tf_op jit(solution)/shard_map/all_to_all | solution.py:86
  50.0 1.4 %shard_map.107 = (bf16[16,16,216]{2,1,0:T(8,128)(2,1)S(1)}, bf16[48,1152]{1,0:T(8,128)(2,1)S(1)}, s32[96,1]{1,0:T(8,128)S(1)}) custom-call(s32[3]{0:T(128)S(1)} %pad_add_fusion.place_ref, bf16[16,120,128]{2,1,0:T(8,128)(2,1)S(1)} %all_to_all.25.near_ref, bf16[64,24,128]{2,1,0:T(8,128)(2,1)S(1)} %all-to-all-done.weights_ref, ...), custom_call_target="tpu_custom_call" | custom-call | tf_op jit(solution)/shard_map/pallas_call | solution.py:397
  51.4 9.3 %all_to_all.26.pooled_ref = bf16[16,16,216]{2,1,0:T(8,128)(2,1)S(1)} all-to-all(bf16[16,16,216]{2,1,0:T(8,128)(2,1)S(1)} %get-tuple-element.26), channel_id=1, replica_groups=mesh['yh'=4,'core'=2,'yl'=2,'x'=4,'z'=8] {'core','yl','x'}, dimensions={0} | all-to-all | bytes 221184 | tf_op jit(solution)/shard_map/all_to_all | solution.py:86
  60.7 0.8 shard_map.108
  61.6 23.9 %all_to_all.27.far_ref = bf16[32,56,128]{2,1,0:T(8,128)(2,1)S(1)} all-to-all(bf16[32,56,128]{2,1,0:T(8,128)(2,1)S(1)} %get-tuple-element.28), channel_id=1, replica_groups=mesh['yh'=4,'core'=2,'yl'=2,'x'=4,'z'=8] {'yh','z'}, dimensions={0} | all-to-all | bytes 917504 | tf_op jit(solution)/shard_map/all_to_all | solution.py:86
  85.5 1.4 %shard_map.109 = bf16[16,56,128]{2,1,0:T(8,128)(2,1)S(1)} custom-call(f32[2]{0:T(128)S(1)} %pad_maximum_fusion.params_ref, s32[3]{0:T(128)S(1)} %pad_add_fusion.place_ref, bf16[32,56,128]{2,1,0:T(8,128)(2,1)S(1)} %all_to_all.27.far_ref, bf16[48,1152]{1,0:T(8,128)(2,1)S(1)} %get-tuple-element.29.text_ref, bf16[48,1152]{1,0:T(8,128)(2,1)S(1)} %get-tuple-element.30.low_ref, ...), custom_call_target="tpu_custom_call" | custom-call | tf_op jit(solution)/shard_map/pallas_call | solution.py:428
  86.8 11.3 %all_to_all.28.parts_ref = bf16[16,56,128]{2,1,0:T(8,128)(2,1)S(1)} all-to-all(bf16[16,56,128]{2,1,0:T(8,128)(2,1)S(1)} %shard_map.109), channel_id=1, replica_groups=mesh['yh'=4,'core'=2,'yl'=2,'x'=4,'z'=8] {'core','yl','x'}, dimensions={0} | all-to-all | bytes 458752 | tf_op jit(solution)/shard_map/all_to_all | solution.py:86
  98.2 0.8 shard_map.110
  (9 shorter events, 0.1 us)
Async XLA Ops:
  0.6 22.0 %copy-start = (s32[1,768]{1,0:T(1,128)S(1)}, s32[1,768]{1,0:T(1,128)}, u32[]{:S(2)}) copy-start(s32[1,768]{1,0:T(1,128)} %segments_hbm.1) | copy-start | bytes 9220
  2.6 30.1 %all-to-all-start = ((bf16[64,24,128]{2,1,0:T(8,128)(2,1)}), bf16[64,24,128]{2,1,0:T(8,128)(2,1)S(1)}, u32[]{:S(2)}, u32[]{:S(2)}) async-start(bf16[64,24,128]{2,1,0:T(8,128)(2,1)} %shard_map.104), calls=%async_computation | async-start | bytes 786432 | tf_op jit(solution)/shard_map/all_to_all | solution.py:86

commit v7 on v6

--- a/solution.py
+++ b/solution.py
@@ -22,7 +22,6 @@
 FINE = ("yh", "core", "yl", "x", "z")
 FINE_SHAPE = (4, 2, 2, 4, 8)
 SIDE = ("core", "yl", "x")
-FAR = ("yh", "z")
 GRP = ("yl", "x", "z")
 N_SIDE = 16
 N_FAR = 32
@@ -84,6 +83,12 @@
 
 def exchange(blocks, axes):
     return lax.all_to_all(blocks, axes, 0, 0)
+
+
+def far_exchange(blocks):
+    snake = [yh * 128 + (z if yh % 2 == 0 else 7 - z) for yh in range(4) for z in range(8)]
+    groups = [[far + side * 8 for far in snake] for side in range(N_SIDE)]
+    return lax.all_to_all(blocks, FINE, 0, 0, axis_index_groups=groups)
 
 
 def weight_kernel(core_ref, key_hbm, value_hbm, query_hbm, out_ref, key_ref, value_ref, query_ref, tile, sems):
@@ -298,7 +303,8 @@
     columns = IMG_DEV * N_FAR
     column = iota((1, columns), 1)
     device = column % N_FAR
-    device = ((device // 8) * N_SIDE + place_ref[2]) * 8 + device % 8
+    turn = device // 8
+    device = (turn * N_SIDE + place_ref[2]) * 8 + jnp.where(turn % 2 == 0, device % 8, 7 - device % 8)
     text_index = device * IMG_DEV + column // N_FAR
     sums[...] = jnp.zeros_like(sums)
     for first, near, index, place in ((0, text_ref[...], ids, 0), (IMG_DEV, low_ref[...], text_index, 1)):
@@ -479,7 +485,7 @@
     pooled, texts, index = pooled_messages(place, near, weights, query)
     pooled = exchange(pooled, SIDE)
     far, lows, unit_image, image_norm = unit_messages(place, pooled, far_tail)
-    far = exchange(far, FAR)
+    far = far_exchange(far)
     parts = exchange(pair_messages(params, place, far, texts, lows, index), SIDE)
     return gradients(parts, unit_text, text_norm, unit_image, image_norm)
 

time: 99.5 us -> 100 us (level)
    all_to_all x0 -> x1, blocking collectives: none -> 24.8 us  [far_exchange(): return lax.all_to_all(blocks, FINE, 0, 0, axis_index_groups=groups)]
    all_to_all x4 -> x3, blocking collectives: 59.8 us -> 35.9 us  [exchange(): return lax.all_to_all(blocks, axes, 0, 0)]
  transfers between devices with their start and end apart: 1 -> 1, of which waited for: 1 -> 1; matrix products, arithmetic and copies ran while one was open for 4% -> 4% of each run, Pallas kernels for 2% -> 1%
where the time goes in v7:
time: 100 us; the launch traced here: 99.8 us
  blocking collectives  60.7 us (61%)
  starting transfers between devices  15.4 us (15%)
  Pallas kernels  9.73 us (10%)
  waiting for transfers between devices  8.28 us (8%)
  other arithmetic  3.44 us (3%)
  between operations  2.07 us (2%)
    all_to_all x3, blocking collectives, exchange(): return lax.all_to_all(blocks, axes, 0, 0)  35.9 us
    all_to_all x1, blocking collectives, far_exchange(): return lax.all_to_all(blocks, FINE, 0, 0, axis_index_groups=groups)  24.8 us
    all_to_all x1, starting transfers between devices, exchange(): return lax.all_to_all(blocks, axes, 0, 0)  15.4 us
    all_to_all x1, waiting for transfers between devices, exchange(): return lax.all_to_all(blocks, axes, 0, 0)  8.28 us
  transfers between devices with their start and end apart: 1, of which 1 were waited for; matrix products, arithmetic and copies ran while one was open for 4% of the time, Pallas kernels for 1%

profile of v7, /device:TPU:1, one launch (start us, length us, event | category | flops | bytes accessed | tf_op | source)
XLA Modules:
  0.0 99.8 jit_solution(6068844775465686645)
XLA Ops:
  0.6 0.0 copy-start
  0.6 2.0 %shard_map.104 = bf16[64,24,128]{2,1,0:T(8,128)(2,1)} custom-call(s32[1]{0:T(128)} %bitcast.core_ref, bf16[18,1152]{1,0:T(8,128)(2,1)} %key_hbm.1, bf16[18,1152]{1,0:T(8,128)(2,1)} %value_hbm.1, bf16[9,128]{1,0:T(8,128)(2,1)} %bitcast.13), custom_call_target="tpu_custom_call" | custom-call | tf_op jit(solution)/shard_map/pallas_call | solution.py:357
  2.6 15.4 %all-to-all-start = ((bf16[64,24,128]{2,1,0:T(8,128)(2,1)}), bf16[64,24,128]{2,1,0:T(8,128)(2,1)S(1)}, u32[]{:S(2)}, u32[]{:S(2)}) async-start(bf16[64,24,128]{2,1,0:T(8,128)(2,1)} %shard_map.104), calls=%async_computation | async-start | bytes 786432 | tf_op jit(solution)/shard_map/all_to_all | solution.py:85
  18.0 0.8 fusion
  18.8 0.8 fusion.1
  21.0 0.8 bitcast_convert_fusion.query_ref
  21.8 0.7 and_select_fusion.1
  22.5 0.1 pad.22.clone
  22.5 0.1 add_convert_fusion
  22.6 0.0 copy-done
  22.6 1.5 %shard_map.105 = (bf16[768,1152]{1,0:T(8,128)(2,1)S(1)}, s32[1,768]{1,0:T(1,128)S(1)}) custom-call(bf16[768,1152]{1,0:T(8,128)(2,1)} %patches_hbm.1, s32[1,768]{1,0:T(1,128)S(1)} %copy-done), custom_call_target="tpu_custom_call" | custom-call | tf_op jit(solution)/shard_map/pallas_call | solution.py:384
  24.1 0.1 pad_maximum_fusion.params_ref
  24.2 0.1 pad_add_fusion.place_ref
  24.3 0.1 maximum_maximum_fusion.tail_ref
  24.4 0.1 broadcast_select_fusion.tail_ref
  24.4 8.3 %all-to-all-done.weights_ref = bf16[64,24,128]{2,1,0:T(8,128)(2,1)S(1)} async-done(((bf16[64,24,128]{2,1,0:T(8,128)(2,1)}), bf16[64,24,128]{2,1,0:T(8,128)(2,1)S(1)}, u32[]{:S(2)}, u32[]{:S(2)}) %all-to-all-start) | async-done | bytes 393248 | tf_op jit(solution)/shard_map/all_to_all | solution.py:85
  32.7 0.1 broadcast_in_dim.38.text_norm_ref
  32.8 1.9 %shard_map.106 = bf16[16,120,128]{2,1,0:T(8,128)(2,1)S(1)} custom-call(bf16[64,24,128]{2,1,0:T(8,128)(2,1)S(1)} %all-to-all-done.weights_ref, bf16[768,1152]{1,0:T(8,128)(2,1)S(1)} %get-tuple-element.22.patches_ref, s32[1,768]{1,0:T(1,128)S(1)} %get-tuple-element.23.segments_ref, f32[117,128]{1,0:T(8,128)S(1)} %broadcast_select_fusion.tail_ref), custom_call_target="tpu_custom_call" | custom-call | tf_op jit(solution)/shard_map/pallas_call | solution.py:394
  34.7 15.3 %all_to_all.25.near_ref = bf16[16,120,128]{2,1,0:T(8,128)(2,1)S(1)} all-to-all(bf16[16,120,128]{2,1,0:T(8,128)(2,1)S(1)} %shard_map.106), channel_id=1, replica_groups=mesh['yh'=4,'core'=2,'yl'=2,'x'=4,'z'=8] {'core','yl','x'}, dimensions={0} | all-to-all | bytes 983040 | tf_op jit(solution)/shard_map/all_to_all | solution.py:85
  50.0 1.4 %shard_map.107 = (bf16[16,16,216]{2,1,0:T(8,128)(2,1)S(1)}, bf16[48,1152]{1,0:T(8,128)(2,1)S(1)}, s32[96,1]{1,0:T(8,128)S(1)}) custom-call(s32[3]{0:T(128)S(1)} %pad_add_fusion.place_ref, bf16[16,120,128]{2,1,0:T(8,128)(2,1)S(1)} %all_to_all.25.near_ref, bf16[64,24,128]{2,1,0:T(8,128)(2,1)S(1)} %all-to-all-done.weights_ref, ...), custom_call_target="tpu_custom_call" | custom-call | tf_op jit(solution)/shard_map/pallas_call | solution.py:403
  51.4 9.3 %all_to_all.26.pooled_ref = bf16[16,16,216]{2,1,0:T(8,128)(2,1)S(1)} all-to-all(bf16[16,16,216]{2,1,0:T(8,128)(2,1)S(1)} %get-tuple-element.26), channel_id=1, replica_groups=mesh['yh'=4,'core'=2,'yl'=2,'x'=4,'z'=8] {'core','yl','x'}, dimensions={0} | all-to-all | bytes 221184 | tf_op jit(solution)/shard_map/all_to_all | solution.py:85
  60.7 0.8 shard_map.108
  61.6 24.8 %all_to_all.27.far_ref = bf16[32,56,128]{2,1,0:T(8,128)(2,1)S(1)} all-to-all(bf16[32,56,128]{2,1,0:T(8,128)(2,1)S(1)} %get-tuple-element.28), channel_id=1, replica_groups={{0,1,2,3,4,5,6,7,135,134,133,132,131,130,129,128,256,257,258,259,260,26..., dimensions={0} | all-to-all | bytes 917504 | tf_op jit(solution)/shard_map/all_to_all | solution.py:91
  86.4 1.4 %shard_map.109 = bf16[16,56,128]{2,1,0:T(8,128)(2,1)S(1)} custom-call(f32[2]{0:T(128)S(1)} %pad_maximum_fusion.params_ref, s32[3]{0:T(128)S(1)} %pad_add_fusion.place_ref, bf16[32,56,128]{2,1,0:T(8,128)(2,1)S(1)} %all_to_all.27.far_ref, bf16[48,1152]{1,0:T(8,128)(2,1)S(1)} %get-tuple-element.29.text_ref, bf16[48,1152]{1,0:T(8,128)(2,1)S(1)} %get-tuple-element.30.low_ref, ...), custom_call_target="tpu_custom_call" | custom-call | tf_op jit(solution)/shard_map/pallas_call | solution.py:434
  87.8 11.3 %all_to_all.28.parts_ref = bf16[16,56,128]{2,1,0:T(8,128)(2,1)S(1)} all-to-all(bf16[16,56,128]{2,1,0:T(8,128)(2,1)S(1)} %shard_map.109), channel_id=1, replica_groups=mesh['yh'=4,'core'=2,'yl'=2,'x'=4,'z'=8] {'core','yl','x'}, dimensions={0} | all-to-all | bytes 458752 | tf_op jit(solution)/shard_map/all_to_all | solution.py:85
  99.0 0.8 shard_map.110
  (9 shorter events, 0.1 us)
Async XLA Ops:
  0.6 22.0 %copy-start = (s32[1,768]{1,0:T(1,128)S(1)}, s32[1,768]{1,0:T(1,128)}, u32[]{:S(2)}) copy-start(s32[1,768]{1,0:T(1,128)} %segments_hbm.1) | copy-start | bytes 9220
  2.6 30.1 %all-to-all-start = ((bf16[64,24,128]{2,1,0:T(8,128)(2,1)}), bf16[64,24,128]{2,1,0:T(8,128)(2,1)S(1)}, u32[]{:S(2)}, u32[]{:S(2)}) async-start(bf16[64,24,128]{2,1,0:T(8,128)(2,1)} %shard_map.104), calls=%async_computation | async-start | bytes 786432 | tf_op jit(solution)/shard_map/all_to_all | solution.py:85

commit v8 on v6

--- a/solution.py
+++ b/solution.py
@@ -37,11 +37,10 @@
 TOPS = 2
 AT_TOP = IMG_DEV
 AT_TEXT = AT_TOP + TOPS * IMG_DEV
-AT_ID = AT_TEXT + IMG_DEV
-NEAR_LIST = AT_ID + 1
-NEAR_ROWS = 120
-AT_NEAR_ID = AT_ID
-AT_SCALAR = NEAR_LIST + AT_ID
+NEAR_LIST = AT_TEXT + IMG_DEV
+AT_NEAR_ID = TILES * NEAR_LIST
+AT_SCALAR = AT_NEAR_ID + 1
+NEAR_ROWS = 112
 N_LANES = 8
 
 AT_FAR_ID = 6 * TILES
@@ -176,8 +175,10 @@
             put(tile * NEAR_LIST + row, context[row * HEADS : (row + 1) * HEADS, tile * 128 : (tile + 1) * 128])
         for row in range(AT_TEXT, NEAR_LIST):
             at = tile * NEAR_LIST + row
-            put(at, scalars if at == AT_SCALAR else jnp.broadcast_to(tail_ref[at : at + 1, :], (HEADS, 128)))
-    for row in range(TILES * NEAR_LIST, NEAR_ROWS):
+            put(at, jnp.broadcast_to(tail_ref[at : at + 1, :], (HEADS, 128)))
+    put(AT_NEAR_ID, jnp.broadcast_to(tail_ref[AT_NEAR_ID : AT_NEAR_ID + 1, :], (HEADS, 128)))
+    put(AT_SCALAR, scalars)
+    for row in range(AT_SCALAR + 1, NEAR_ROWS):
         put(row, blank)
     out_ref[...] = sums[...].reshape(HEADS, NEAR_ROWS, 128).astype(bf16)
 
@@ -199,7 +200,7 @@
 
     near = jnp.concatenate(
         [
-            jnp.concatenate([take(tile * NEAR_LIST + row) for row in range(AT_ID)], axis=0).astype(bf16)
+            jnp.concatenate([take(tile * NEAR_LIST + row) for row in range(NEAR_LIST)], axis=0).astype(bf16)
             for tile in range(TILES)
         ],
         axis=1,
@@ -463,8 +464,8 @@
     text_norm = jnp.broadcast_to(text_norm, (IMG_DEV, 128))
     text_low = tiled_rows(lax.reduce_precision(unit_text, 8, 7))
     ids = code_ids(image_ids)
-    near_tail = jnp.pad(text_low, ((0, 0), (AT_TEXT, 1), (0, 0))).reshape(TILES * NEAR_LIST, 128)
-    near_tail = jnp.where(jnp.arange(TILES * NEAR_LIST)[:, None] == AT_NEAR_ID, ids, near_tail)
+    near_tail = jnp.pad(text_low, ((0, 0), (AT_TEXT, 0), (0, 0))).reshape(AT_NEAR_ID, 128)
+    near_tail = jnp.concatenate([near_tail, ids], axis=0)
     far_tail = jnp.pad(text_low, ((0, 0), (IMG_DEV, 0), (0, 0))).reshape(6 * TILES, 128)
     far_tail = jnp.concatenate([far_tail, ids, jnp.zeros((1, 128), f32)], axis=0)
     query = lax.dynamic_slice_in_dim(pool_query, side * HEAD_DIM, HEAD_DIM)[None].astype(f32)

time: 99.5 us -> 99.2 us (level)
  no operation moved by 1% of the time
where the time goes in v8:
time: 99.2 us; the launch traced here: 98.7 us
  blocking collectives  59.5 us (60%)
  starting transfers between devices  15.4 us (16%)
  Pallas kernels  9.84 us (10%)
  waiting for transfers between devices  8.38 us (8%)
  other arithmetic  3.36 us (3%)
  between operations  2.05 us (2%)
    all_to_all x4, blocking collectives, exchange(): return lax.all_to_all(blocks, axes, 0, 0)  59.5 us
    all_to_all x1, starting transfers between devices, exchange(): return lax.all_to_all(blocks, axes, 0, 0)  15.4 us
    all_to_all x1, waiting for transfers between devices, exchange(): return lax.all_to_all(blocks, axes, 0, 0)  8.38 us
  transfers between devices with their start and end apart: 1, of which 1 were waited for; matrix products, arithmetic and copies ran while one was open for 4% of the time, Pallas kernels for 2%

profile of v8, /device:TPU:1, one launch (start us, length us, event | category | flops | bytes accessed | tf_op | source)
XLA Modules:
  0.0 98.7 jit_solution(13623577177782163015)
XLA Ops:
  0.6 0.0 copy-start
  0.6 2.0 %shard_map.104 = bf16[64,24,128]{2,1,0:T(8,128)(2,1)} custom-call(s32[1]{0:T(128)} %bitcast.core_ref, bf16[18,1152]{1,0:T(8,128)(2,1)} %key_hbm.1, bf16[18,1152]{1,0:T(8,128)(2,1)} %value_hbm.1, bf16[9,128]{1,0:T(8,128)(2,1)} %bitcast.13), custom_call_target="tpu_custom_call" | custom-call | tf_op jit(solution)/shard_map/pallas_call | solution.py:352
  2.6 15.4 %all-to-all-start = ((bf16[64,24,128]{2,1,0:T(8,128)(2,1)}), bf16[64,24,128]{2,1,0:T(8,128)(2,1)S(1)}, u32[]{:S(2)}, u32[]{:S(2)}) async-start(bf16[64,24,128]{2,1,0:T(8,128)(2,1)} %shard_map.104), calls=%async_computation | async-start | bytes 786432 | tf_op jit(solution)/shard_map/all_to_all | solution.py:85
  18.0 0.8 fusion
  18.8 0.8 fusion.1
  21.0 0.8 bitcast_convert_fusion.query_ref
  21.7 0.7 and_select_fusion.1
  22.4 0.1 pad.22.clone
  22.5 0.0 copy-done
  22.5 1.5 %shard_map.105 = (bf16[768,1152]{1,0:T(8,128)(2,1)S(1)}, s32[1,768]{1,0:T(1,128)S(1)}) custom-call(bf16[768,1152]{1,0:T(8,128)(2,1)} %patches_hbm.1, s32[1,768]{1,0:T(1,128)S(1)} %copy-done), custom_call_target="tpu_custom_call" | custom-call | tf_op jit(solution)/shard_map/pallas_call | solution.py:379
  24.0 0.1 add_convert_fusion
  24.1 0.1 pad_maximum_fusion.1.params_ref
  24.2 0.1 pad_add_fusion.place_ref
  24.3 0.1 maximum_maximum_fusion.tail_ref
  24.3 8.4 %all-to-all-done.weights_ref = bf16[64,24,128]{2,1,0:T(8,128)(2,1)S(1)} async-done(((bf16[64,24,128]{2,1,0:T(8,128)(2,1)}), bf16[64,24,128]{2,1,0:T(8,128)(2,1)S(1)}, u32[]{:S(2)}, u32[]{:S(2)}) %all-to-all-start) | async-done | bytes 393248 | tf_op jit(solution)/shard_map/all_to_all | solution.py:85
  32.7 0.1 broadcast_in_dim.19.text_norm_ref
  32.8 2.0 %shard_map.106 = bf16[16,112,128]{2,1,0:T(8,128)(2,1)S(1)} custom-call(bf16[64,24,128]{2,1,0:T(8,128)(2,1)S(1)} %all-to-all-done.weights_ref, bf16[768,1152]{1,0:T(8,128)(2,1)S(1)} %get-tuple-element.22.patches_ref, s32[1,768]{1,0:T(1,128)S(1)} %get-tuple-element.23.segments_ref, f32[109,128]{1,0:T(8,128)S(1)} %pad_maximum_fusion.tail_ref), custom_call_target="tpu_custom_call" | custom-call | tf_op jit(solution)/shard_map/pallas_call | solution.py:389
  34.8 15.0 %all_to_all.25.near_ref = bf16[16,112,128]{2,1,0:T(8,128)(2,1)S(1)} all-to-all(bf16[16,112,128]{2,1,0:T(8,128)(2,1)S(1)} %shard_map.106), channel_id=1, replica_groups=mesh['yh'=4,'core'=2,'yl'=2,'x'=4,'z'=8] {'core','yl','x'}, dimensions={0} | all-to-all | bytes 917504 | tf_op jit(solution)/shard_map/all_to_all | solution.py:85
  49.7 1.5 %shard_map.107 = (bf16[16,16,216]{2,1,0:T(8,128)(2,1)S(1)}, bf16[48,1152]{1,0:T(8,128)(2,1)S(1)}, s32[96,1]{1,0:T(8,128)S(1)}) custom-call(s32[3]{0:T(128)S(1)} %pad_add_fusion.place_ref, bf16[16,112,128]{2,1,0:T(8,128)(2,1)S(1)} %all_to_all.25.near_ref, bf16[64,24,128]{2,1,0:T(8,128)(2,1)S(1)} %all-to-all-done.weights_ref, ...), custom_call_target="tpu_custom_call" | custom-call | tf_op jit(solution)/shard_map/pallas_call | solution.py:398
  51.2 9.3 %all_to_all.26.pooled_ref = bf16[16,16,216]{2,1,0:T(8,128)(2,1)S(1)} all-to-all(bf16[16,16,216]{2,1,0:T(8,128)(2,1)S(1)} %get-tuple-element.26), channel_id=1, replica_groups=mesh['yh'=4,'core'=2,'yl'=2,'x'=4,'z'=8] {'core','yl','x'}, dimensions={0} | all-to-all | bytes 221184 | tf_op jit(solution)/shard_map/all_to_all | solution.py:85
  60.5 0.8 shard_map.108
  61.3 23.9 %all_to_all.27.far_ref = bf16[32,56,128]{2,1,0:T(8,128)(2,1)S(1)} all-to-all(bf16[32,56,128]{2,1,0:T(8,128)(2,1)S(1)} %get-tuple-element.28), channel_id=1, replica_groups=mesh['yh'=4,'core'=2,'yl'=2,'x'=4,'z'=8] {'yh','z'}, dimensions={0} | all-to-all | bytes 917504 | tf_op jit(solution)/shard_map/all_to_all | solution.py:85
  85.2 1.4 %shard_map.109 = bf16[16,56,128]{2,1,0:T(8,128)(2,1)S(1)} custom-call(f32[2]{0:T(128)S(1)} %pad_maximum_fusion.1.params_ref, s32[3]{0:T(128)S(1)} %pad_add_fusion.place_ref, bf16[32,56,128]{2,1,0:T(8,128)(2,1)S(1)} %all_to_all.27.far_ref, bf16[48,1152]{1,0:T(8,128)(2,1)S(1)} %get-tuple-element.29.text_ref, bf16[48,1152]{1,0:T(8,128)(2,1)S(1)} %get-tuple-element.30.low_ref, ...), custom_call_target="tpu_custom_call" | custom-call | tf_op jit(solution)/shard_map/pallas_call | solution.py:429
  86.6 11.3 %all_to_all.28.parts_ref = bf16[16,56,128]{2,1,0:T(8,128)(2,1)S(1)} all-to-all(bf16[16,56,128]{2,1,0:T(8,128)(2,1)S(1)} %shard_map.109), channel_id=1, replica_groups=mesh['yh'=4,'core'=2,'yl'=2,'x'=4,'z'=8] {'core','yl','x'}, dimensions={0} | all-to-all | bytes 458752 | tf_op jit(solution)/shard_map/all_to_all | solution.py:85
  97.9 0.8 shard_map.110
  (9 shorter events, 0.1 us)
Async XLA Ops:
  0.6 21.9 %copy-start = (s32[1,768]{1,0:T(1,128)S(1)}, s32[1,768]{1,0:T(1,128)}, u32[]{:S(2)}) copy-start(s32[1,768]{1,0:T(1,128)} %segments_hbm.1) | copy-start | bytes 9220
  2.6 30.1 %all-to-all-start = ((bf16[64,24,128]{2,1,0:T(8,128)(2,1)}), bf16[64,24,128]{2,1,0:T(8,128)(2,1)S(1)}, u32[]{:S(2)}, u32[]{:S(2)}) async-start(bf16[64,24,128]{2,1,0:T(8,128)(2,1)} %shard_map.104), calls=%async_computation | async-start | bytes 786432 | tf_op jit(solution)/shard_map/all_to_all | solution.py:85
